TPU v7x, 512 devices: a whole 4x8x8 slice. The times are simulated.
512 devices in a mesh: dp: 32 (over y_lo, z), tensor: 16 (over x, y_hi, core).
Axes of the slice: x: 4, y: 8 (y_hi: 2, y_lo: 4; y = y_hi * 4 + y_lo), z: 8, core: 2. Of those that a mesh axis runs over, the one named last changes fastest.
Arguments:
- tokens: bfloat16 [4096, 4096], P(('dp', 'tensor')), may hold values from -6 to 6
- upstream_grad: bfloat16 [4096, 4096], P(('dp', 'tensor')), may hold values from -24 to 24
- w_gate: bfloat16 [4096, 14336], P(None, 'tensor'), may hold values from -0.09375 to 0.09375
- w_up: bfloat16 [4096, 14336], P(None, 'tensor'), may hold values from -0.09375 to 0.09375
- w_down: bfloat16 [14336, 4096], P('tensor'), may hold values from -0.046875 to 0.046875
Outputs:
- grad_tokens: bfloat16 [4096, 4096], P(('dp', 'tensor'))
- grad_down: float32 [14336, 4096], P('tensor', 'dp')
All inputs are finite; a program needn't handle non-finite values.
Results may differ from a plain program's by a relative error of at most 0.03.
Values may be sent and summed in bfloat16 or wider, within the bound.
No kernel may reach another device: no remote copies, remote signals or barrier semaphores. Data moves between devices by JAX's collectives and lax.ppermute only.
A program may use at most 128 MiB of HBM per device.

v0:
```python
import jax
import jax.numpy as jnp
from jax import lax
from jax.sharding import PartitionSpec as P


def contract_rows(left, right):
    return lax.dot_general(
        left, right, (((0,), (0,)), ((), ())), preferred_element_type=jnp.float32
    )


def contract_cols(left, right):
    return lax.dot_general(
        left, right, (((1,), (1,)), ((), ())), preferred_element_type=jnp.float32
    )


def body(tokens, upstream_grad, w_gate, w_up, w_down):
    gathered, upstream = (
        lax.all_gather(tokens, "tensor", axis=0, tiled=True),
        lax.all_gather(upstream_grad, "tensor", axis=0, tiled=True),
    )
    gate_pre = jnp.dot(gathered, w_gate, preferred_element_type=jnp.float32)
    up_pre = jnp.dot(gathered, w_up, preferred_element_type=jnp.float32)
    sig_gate = jax.nn.sigmoid(gate_pre)
    act_gate = gate_pre * sig_gate
    hidden = (act_gate * up_pre).astype(jnp.bfloat16)
    grad_hidden = contract_cols(upstream, w_down).astype(jnp.bfloat16)
    hidden_f = grad_hidden.astype(jnp.float32)
    grad_gate = (hidden_f * up_pre * sig_gate * (1.0 + gate_pre * (1.0 - sig_gate))).astype(
        jnp.bfloat16
    )
    grad_up = (hidden_f * act_gate).astype(jnp.bfloat16)
    total_tokens = upstream.shape[0] * lax.axis_size("dp")
    factor = float(total_tokens) ** (-0.5)
    summed = lax.psum_scatter(
        (contract_cols(grad_gate, w_gate) + contract_cols(grad_up, w_up)).astype(jnp.bfloat16),
        "tensor",
        scatter_dimension=0,
        tiled=True,
    )
    partial_grad = contract_rows(hidden, upstream) * factor
    grad_down = lax.psum_scatter(
        partial_grad.astype(jnp.bfloat16), "dp", scatter_dimension=1, tiled=True
    ).astype(jnp.float32)
    return (summed, grad_down)


def solution(mesh):
    in_specs = (
        P(("dp", "tensor"), None),
        P(("dp", "tensor"), None),
        P(None, "tensor"),
        P(None, "tensor"),
        P("tensor", None),
    )
    out_specs = (P(("dp", "tensor"), None), P("tensor", "dp"))
    return jax.shard_map(body, mesh=mesh, in_specs=in_specs, out_specs=out_specs, check_vma=False)
```

profile of v0, /device:TPU:1, one launch (start us, length us, event | category | flops | bytes accessed | tf_op | source)
XLA Modules:
  0.0 420.7 jit_solution(18364517736532826342)
XLA Ops:
  7.2 0.0 all-gather.5.cloned.1.call-start
  7.2 0.7 all-gather.5.cloned.1.call-update
  7.9 0.0 all-gather.3.cloned.1.call-start
  7.9 0.7 all-gather.3.cloned.1.call-update
  8.6 0.0 reduce-scatter.7.cloned.1.call-start
  8.7 67.9 %all-gather.5.cloned.1.call-done = bf16[128,4096]{1,0:T(8,128)(2,1)} async-done(((bf16[8,4096]{1,0:T(8,128)(2,1)}), bf16[128,4096]{1,0:T(8,128)(2,1)}) %all-gather.5.cloned.1.call-update) | async-done | bytes 1048592 | tf_op jit(solution)/shard_map/all_gather | solution.py:21
  76.6 0.0 copy-start
  76.6 4.8 %fusion.11 = f32[128,896]{1,0:T(8,128)S(1)} fusion(bf16[128,4096]{1,0:T(8,128)(2,1)} %all-gather.5.cloned.1.call-done, bf16[4096,896]{1,0:T(8,128)(2,1)} %param.7), kind=kOutput, calls=%fused_computation.16 | convolution fusion | flops 939524096 | bytes 8847360 | tf_op jit(solution)/shard_map/dot_general | solution.py:24
  81.4 0.0 copy-done
  81.4 4.4 %fusion.10 = f32[128,896]{1,0:T(8,128)S(1)} fusion(bf16[128,4096]{1,0:T(8,128)(2,1)S(1)} %copy-done, bf16[4096,896]{1,0:T(8,128)(2,1)} %param.8), kind=kOutput, calls=%fused_computation.15 | convolution fusion | flops 939524096 | bytes 8847360 | tf_op jit(solution)/shard_map/dot_general | solution.py:25
  85.8 51.0 %all-gather.3.cloned.1.call-done = bf16[128,4096]{1,0:T(8,128)(2,1)} async-done(((bf16[8,4096]{1,0:T(8,128)(2,1)}), bf16[128,4096]{1,0:T(8,128)(2,1)}) %all-gather.3.cloned.1.call-update) | async-done | bytes 1048592 | tf_op jit(solution)/shard_map/all_gather | solution.py:22
  136.7 6.3 %multiply_convert_fusion = bf16[896,4096]{1,0:T(8,128)(2,1)} fusion(bf16[128,4096]{1,0:T(8,128)(2,1)} %all-gather.3.cloned.1.call-done, f32[128,896]{1,0:T(8,128)S(1)} %fusion.10, f32[128,896]{1,0:T(8,128)S(1)} %fusion.11), kind=kOutput, calls=%fused_computation | convolution fusion | flops 947552256 | bytes 9306112 | tf_op jit(solution)/shard_map/dot_general | solution.py:8
  143.1 10.8 %copy.7 = bf16[896,4096]{0,1:T(8,128)(2,1)} copy(bf16[896,4096]{1,0:T(8,128)(2,1)} %multiply_convert_fusion) | data formatting | bytes 14680064
  153.9 0.0 copy-start.1
  153.9 0.0 reduce-scatter.7.cloned.1.call-update
  153.9 0.0 reduce-scatter.5.cloned.1.call-start
  153.9 1.1 copy-done.1
  155.1 0.0 slice-start
  155.1 5.7 %fusion.1 = f32[128,896]{1,0:T(8,128)S(1)} fusion(bf16[128,4096]{1,0:T(8,128)(2,1)S(1)} %copy-done.1, bf16[896,4096]{1,0:T(8,128)(2,1)} %param.9), kind=kOutput, calls=%fused_computation.4 | convolution fusion | flops 939753472 | bytes 8847360 | tf_op jit(solution)/shard_map/dot_general | solution.py:14
  160.8 0.0 slice-start.1
  160.8 5.7 %fusion.3 = f32[128,4096]{1,0:T(8,128)S(1)} fusion(bf16[4096,896]{1,0:T(8,128)(2,1)} %param.7, f32[128,896]{1,0:T(8,128)S(1)} %fusion.11, f32[128,896]{1,0:T(8,128)S(1)} %fusion.1, f32[128,896]{1,0:T(8,128)S(1)} %fusion.10), kind=kOutput, calls=%fused_computation.10 | convolution fusion | flops 940670976 | bytes 10813440 | tf_op jit(solution)/shard_map/dot_general | solution.py:14
  166.5 0.0 slice-done
  166.5 0.0 slice-done.1
  166.5 3.5 fusion
  170.0 0.0 reduce-scatter.5.cloned.1.call-update
  170.0 135.9 %reduce-scatter.7.cloned.1.call-done = bf16[128,896]{1,0:T(8,128)(2,1)} async-done(((bf16[4096,896]{1,0:T(8,128)(2,1)}), bf16[128,896]{1,0:T(8,128)(2,1)}) %reduce-scatter.7.cloned.1.call-update) | async-done | bytes 229392
  305.9 1.1 copy.8
  307.0 0.8 convert_element_type.31
  307.8 106.4 %reduce-scatter.5.cloned.1.call-done = bf16[8,4096]{1,0:T(8,128)(2,1)} async-done(((bf16[128,4096]{1,0:T(8,128)(2,1)}), bf16[8,4096]{1,0:T(8,128)(2,1)}) %reduce-scatter.5.cloned.1.call-update) | async-done | bytes 65552 | tf_op jit(solution)/shard_map/reduce_scatter | solution.py:37
  (1 shorter events, 0.0 us)
Async XLA Ops:
  7.2 69.5 %all-gather.5.cloned.1.call-start = ((), (), s32[]{:S(2)}) async-start(), calls=%async_computation.3 | async-start | bytes 1114112 | tf_op jit(solution)/shard_map/all_gather | solution.py:21
  7.9 128.8 %all-gather.3.cloned.1.call-start = ((), (), s32[]{:S(2)}) async-start(), calls=%async_computation.2 | async-start | bytes 1114112 | tf_op jit(solution)/shard_map/all_gather | solution.py:22
  8.6 297.2 %reduce-scatter.7.cloned.1.call-start = ((), (), s32[]{:S(2)}) async-start(), calls=%async_computation.5 | async-start | bytes 7569408
  76.6 4.8 %copy-start = (bf16[128,4096]{1,0:T(8,128)(2,1)S(1)}, bf16[128,4096]{1,0:T(8,128)(2,1)}, u32[]{:S(2)}) copy-start(bf16[128,4096]{1,0:T(8,128)(2,1)} %all-gather.5.cloned.1.call-done) | copy-start | bytes 3145732
  153.9 1.2 copy-start.1
  153.9 260.2 %reduce-scatter.5.cloned.1.call-start = ((), (), s32[]{:S(2)}) async-start(), calls=%async_computation.4 | async-start | bytes 1114112 | tf_op jit(solution)/shard_map/reduce_scatter | solution.py:37
  155.1 11.4 %slice-start = ((s8[7340032]{0:T(1024)(128)(4,1)}), s8[4194304]{0:T(1024)(128)(4,1)S(1)}, s32[]{:S(2)}) async-start(s8[7340032]{0:T(1024)(128)(4,1)} %bitcast.11), calls=%async_computation.6 | async-start | bytes 8388608
  160.8 5.7 %slice-start.1 = ((s8[7340032]{0:T(1024)(128)(4,1)}), s8[3145728]{0:T(1024)(128)(4,1)S(1)}, s32[]{:S(2)}) async-start(s8[7340032]{0:T(1024)(128)(4,1)} %bitcast.11), calls=%async_computation.7 | async-start | bytes 6291456
Sparse Core Ops, SparseCore 0:
  11.3 65.3 all-gather.4
  79.9 56.8 all-gather.2
  154.0 151.8 reduce-scatter.6
  311.0 103.0 reduce-scatter.4
where the time goes:
time: 421 us
  waiting for transfers between devices  363 us (86%)
  matrix products  30.3 us (7%)
  between operations  13.8 us (3%)
  local copies, waits for them, and re-layouts  13 us (3%)
    unnamed x5, waiting for transfers between devices  137 us
    reduce_scatter x1, waiting for transfers between devices, body(): lax.psum_scatter((contract_cols(grad_gate, w_gate) + contract_cols(grad_u...  106 us
    all_gather x1, waiting for transfers between devices, body(): lax.all_gather(tokens, 'tensor', axis=0, tiled=True)  67.9 us
    all_gather x1, waiting for transfers between devices, body(): lax.all_gather(upstream_grad, 'tensor', axis=0, tiled=True)  51 us
    dot_general x3, matrix products, contract_cols(): lax.dot_general(left, right, (((1,), (1,)), ((), ())), preferred_element_...  14.8 us
    unnamed x10, local copies, waits for them, and re-layouts  13 us
  transfers between devices with their start and end apart: 4, of which 4 were waited for; matrix products, arithmetic and copies ran while one was open for 6% of the time, Pallas kernels for 0%

commit v1 on v0

v1 whole, which is shorter than its diff:
```python
import jax
import jax.numpy as jnp
from jax import lax
from jax.sharding import Mesh, PartitionSpec as P

SIZES = (4, 8, 4, 2, 2)
NAMES = ("ylo", "z", "x", "yhi", "core")
SWAP = [(0, 1), (1, 0)]


def contract_rows(left, right):
    return lax.dot_general(
        left, right, (((0,), (0,)), ((), ())), preferred_element_type=jnp.float32
    )


def contract_cols(left, right):
    return lax.dot_general(
        left, right, (((1,), (1,)), ((), ())), preferred_element_type=jnp.float32
    )


def swap(value, axis):
    return lax.ppermute(value, axis, SWAP)


def both(rows, axis):
    return jnp.concatenate([rows, swap(rows, axis)], axis=0)


def gather_a2a(rows, axis):
    n = lax.axis_size(axis)
    copies = jnp.broadcast_to(rows[None], (n,) + rows.shape)
    return lax.all_to_all(copies, axis, 0, 0).reshape((n * rows.shape[0],) + rows.shape[1:])


def after(value, *earlier):
    return lax.optimization_barrier((value,) + earlier)[0]


def body(tokens, upstream_grad, w_gate, w_up, w_down):
    rows, width = tokens.shape
    f_dev = w_gate.shape[1]
    n_y, n_z, n_x = lax.axis_size("ylo"), lax.axis_size("z"), lax.axis_size("x")
    block = width // (n_y * n_z)

    tokens2 = both(tokens, "yhi")
    upstream2 = both(upstream_grad, "yhi")
    cols = upstream_grad.reshape(rows, n_y, n_z, block).transpose(2, 0, 1, 3)
    cols = cols.reshape(n_z * rows, n_y * block)
    cols = lax.all_to_all(cols, "z", 0, 0, tiled=True)
    cols2 = both(cols, "yhi")

    tokens_x = lax.all_gather(tokens2, "x", axis=0, tiled=True)
    upstream_x = gather_a2a(after(upstream2, tokens_x), "x")
    gathered = both(tokens_x, "core")
    gate_pre = jnp.dot(gathered, w_gate, preferred_element_type=jnp.float32)
    up_pre = jnp.dot(gathered, w_up, preferred_element_type=jnp.float32)
    sig_gate = jax.nn.sigmoid(gate_pre)
    act_gate = gate_pre * sig_gate
    hidden = (act_gate * up_pre).astype(jnp.bfloat16)
    hidden_z = gather_a2a(after(hidden, upstream_x), "z")

    upstream = both(after(upstream_x, hidden), "core")
    grad_hidden = contract_cols(upstream, w_down).astype(jnp.bfloat16)
    hidden_f = grad_hidden.astype(jnp.float32)
    grad_gate = (hidden_f * up_pre * sig_gate * (1.0 + gate_pre * (1.0 - sig_gate))).astype(
        jnp.bfloat16
    )
    grad_up = (hidden_f * act_gate).astype(jnp.bfloat16)
    partial = (contract_cols(grad_gate, w_gate) + contract_cols(grad_up, w_up)).astype(jnp.bfloat16)

    half = partial.shape[0] // 2
    other = swap(partial[half:], "core")
    partial = (partial[:half].astype(jnp.float32) + other.astype(jnp.float32)).astype(jnp.bfloat16)

    cols = both(lax.all_gather(after(cols2, hidden), "x", axis=0, tiled=True), "core")
    n_t = cols.shape[0] // (n_z * rows)
    cols = cols.reshape(n_t, n_z, rows, n_y * block).transpose(1, 0, 2, 3)
    cols = cols.reshape(n_z * n_t * rows, n_y * block)
    factor = float(n_z * n_t * rows * n_y) ** (-0.5)
    parts = [
        (contract_rows(hidden_z, cols[:, i * block : (i + 1) * block]) * factor).astype(jnp.bfloat16)
        for i in range(n_y)
    ]
    down = lax.all_to_all(jnp.concatenate(parts, axis=0), "ylo", 0, 0, tiled=True)

    me = lax.axis_index("x")
    chunk = 2 * rows
    total = lax.dynamic_slice_in_dim(partial, me * chunk, chunk, 0).astype(jnp.float32)
    for k in range(1, n_x):
        piece = lax.dynamic_slice_in_dim(partial, lax.rem(me + k, n_x) * chunk, chunk, 0)
        piece = lax.ppermute(piece, "x", [(i, (i + k) % n_x) for i in range(n_x)])
        total = total + piece.astype(jnp.float32)
    other = swap(total[rows:].astype(jnp.bfloat16), "yhi")
    summed = (total[:rows] + other.astype(jnp.float32)).astype(jnp.bfloat16)

    grad_down = down.reshape(n_y, f_dev, block).astype(jnp.float32).sum(0)
    return (summed, grad_down)


def solution(mesh):
    cut = Mesh(mesh.devices.reshape(SIZES), NAMES)
    dp, tensor = NAMES[:2], NAMES[2:]
    in_specs = (
        P(dp + tensor, None),
        P(dp + tensor, None),
        P(None, tensor),
        P(None, tensor),
        P(tensor, None),
    )
    out_specs = (P(dp + tensor, None), P(tensor, dp))
    return jax.shard_map(body, mesh=cut, in_specs=in_specs, out_specs=out_specs, check_vma=False)
```

time: 421 us -> 166 us (0.39)
  waiting for transfers between devices: 363 us -> 23.1 us
  starting transfers between devices: 0.16 us -> 67.5 us
  blocking collectives: 0 us -> 36.3 us
  between operations: 13.8 us -> 1.09 us
  local copies, waits for them, and re-layouts: 13 us -> 3.39 us
  other arithmetic: 0.8 us -> 5.71 us
    unnamed x5 -> x0, waiting for transfers between devices: 137 us -> none
    all_gather x2 -> x0, waiting for transfers between devices: 119 us -> none  [the longest x1 67.9 us: body(): lax.all_gather(tokens, 'tensor', axis=0, tiled=True)]
    reduce_scatter x1 -> x0, waiting for transfers between devices: 106 us -> none  [body(): lax.psum_scatter((contract_cols(grad_gate, w_gate) + contract_cols(grad_u...]
    ppermute x0 -> x11, starting transfers between devices: none -> 55.4 us  [the longest x8 47.4 us: swap(): return lax.ppermute(value, axis, SWAP)]
    all_gather x0 -> x2, blocking collectives: none -> 22.9 us  [the longest x1 12.1 us: body(): lax.all_gather(after(cols2, hidden), 'x', axis=0, tiled=True)]
    ppermute x0 -> x11, waiting for transfers between devices: none -> 15.9 us  [the longest x8 15.9 us: swap(): return lax.ppermute(value, axis, SWAP)]
    all_to_all x0 -> x1, blocking collectives: none -> 13.4 us  [body(): cols = lax.all_to_all(cols, 'z', 0, 0, tiled=True)]
    unnamed x10 -> x22, local copies, waits for them, and re-layouts: 13 us -> 0.86 us
  transfers between devices with their start and end apart: 4 -> 14, of which waited for: 4 -> 6; matrix products, arithmetic and copies ran while one was open for 6% -> 21% of each run, Pallas kernels for 0% -> 0%
where the time goes in v1:
time: 166 us; the launch traced here: 163 us
  starting transfers between devices  67.5 us (41%)
  blocking collectives  36.3 us (22%)
  matrix products  26.3 us (16%)
  waiting for transfers between devices  23.1 us (14%)
  other arithmetic  5.71 us (3%)
  local copies, waits for them, and re-layouts  3.39 us (2%)
    ppermute x8, starting transfers between devices, swap(): return lax.ppermute(value, axis, SWAP)  47.4 us
    ppermute x8, waiting for transfers between devices, swap(): return lax.ppermute(value, axis, SWAP)  15.9 us
    all_to_all x1, blocking collectives, body(): cols = lax.all_to_all(cols, 'z', 0, 0, tiled=True)  13.4 us
    all_gather x1, blocking collectives, body(): lax.all_gather(after(cols2, hidden), 'x', axis=0, tiled=True)  12.1 us
    dot_general x3, matrix products, contract_cols(): lax.dot_general(left, right, (((1,), (1,)), ((), ())), preferred_element_...  10.9 us
    all_gather x1, blocking collectives, body(): tokens_x = lax.all_gather(tokens2, 'x', axis=0, tiled=True)  10.8 us
    dot_general x4, matrix products, contract_rows(): lax.dot_general(left, right, (((0,), (0,)), ((), ())), preferred_element_...  8.76 us
    all_to_all x2, starting transfers between devices, gather_a2a(): lax.all_to_all(copies, axis, 0, 0)  8.59 us
  transfers between devices with their start and end apart: 14, of which 6 were waited for; matrix products, arithmetic and copies ran while one was open for 21% of the time, Pallas kernels for 0%

profile of v1, /device:TPU:1, one launch (start us, length us, event | category | flops | bytes accessed | tf_op | source)
XLA Modules:
  0.0 163.3 jit_solution(14229515356374131774)
XLA Ops:
  0.6 8.3 %collective-permute-start.1 = (bf16[8,4096]{1,0:T(8,128)(2,1)}, bf16[8,4096]{1,0:T(8,128)(2,1)S(1)}, u32[]{:S(2)}, u32[]{:S(2)}) collective-permute-start(bf16[8,4096]{1,0:T(8,128)(2,1)} %param.5), channel_id=1, source_target_pairs={{0,2},{2,0},{1,3},{3,1},{4,6},{6,4},{5,7},{7,5},{8,10},{10,8},{9,1... | collective-permute-start | bytes 196616 | tf_op jit(solution)/shard_map/ppermute | solution.py:24
  8.9 1.9 %collective-permute-start = (bf16[8,4096]{1,0:T(8,128)(2,1)}, bf16[8,4096]{1,0:T(8,128)(2,1)S(1)}, u32[]{:S(2)}, u32[]{:S(2)}) collective-permute-start(bf16[8,4096]{1,0:T(8,128)(2,1)} %param.6), channel_id=1, source_target_pairs={{0,2},{2,0},{1,3},{3,1},{4,6},{6,4},{5,7},{7,5},{8,10},{10,8},{9,1... | collective-permute-start | bytes 196616 | tf_op jit(solution)/shard_map/ppermute | solution.py:24
  11.7 10.8 %all_gather.6 = bf16[64,4096]{1,0:T(8,128)(2,1)S(1)} all-gather(bf16[16,4096]{1,0:T(8,128)(2,1)S(1)} %pad_maximum_fusion.3), channel_id=1, replica_groups=mesh['ylo'=4,'z'=8,'x'=4,'yhi'=2,'core'=2] {'x'}, dimensions={0}, use_global_device_ids=true | all-gather | bytes 655360 | tf_op jit(solution)/shard_map/all_gather | solution.py:54
  22.5 10.9 %collective-permute-start.2 = (bf16[64,4096]{1,0:T(8,128)(2,1)S(1)}, bf16[64,4096]{1,0:T(8,128)(2,1)S(1)}, u32[]{:S(2)}, u32[]{:S(2)}) collective-permute-start(bf16[64,4096]{1,0:T(8,128)(2,1)S(1)} %all_gather.6), channel_id=1, source_target_pairs={{0,1},{1,0},{2,3},{3,2},{4,5},{5,4},{6,7},{7,6},{8,9},{9,8},{10,11... | collective-permute-start | bytes 1572872 | tf_op jit(solution)/shard_map/ppermute | solution.py:24
  35.1 4.1 %all-to-all-start = ((bf16[4,16,4096]{2,1,0:T(8,128)(2,1)}), bf16[4,16,4096]{2,1,0:T(8,128)(2,1)}, u32[]{:S(2)}, u32[]{:S(2)}) async-start(bf16[4,16,4096]{2,1,0:T(8,128)(2,1)} %broadcast_in_dim.4), calls=%async_computation | async-start | bytes 1048576 | tf_op jit(solution)/shard_map/all_to_all | solution.py:34
  39.4 4.5 %fusion.21 = f32[128,896]{1,0:T(8,128)S(1)} fusion(bf16[128,4096]{1,0:T(8,128)(2,1)S(1)} %constant_dynamic-update-slice_fusion, bf16[4096,896]{1,0:T(8,128)(2,1)} %param.7), kind=kOutput, calls=%fused_computation.47 | convolution fusion | flops 939524096 | bytes 8847360 | tf_op jit(solution)/shard_map/dot_general | solution.py:57
  44.7 2.1 %multiply_convert_fusion.2 = (bf16[128,896]{1,0:T(8,128)(2,1)S(1)}, f32[128,896]{1,0:T(8,128)}) fusion(f32[128,896]{1,0:T(8,128)S(1)} %fusion.21, bf16[128,4096]{1,0:T(8,128)(2,1)S(1)} %constant_dynamic-update-slice_fusion, bf16[4096,896]{1,0:T(8,128)(2,1)S(1)} %bitcast.33), kind=kOutput, calls=%fused_computation.21 | convolution fusion | flops 940212224 | bytes 9535488 | tf_op jit(solution)/shard_map/dot_general | solution.py:58
  46.8 2.2 %all-to-all-done = bf16[4,16,4096]{2,1,0:T(8,128)(2,1)} async-done(((bf16[4,16,4096]{2,1,0:T(8,128)(2,1)}), bf16[4,16,4096]{2,1,0:T(8,128)(2,1)}, u32[]{:S(2)}, u32[]{:S(2)}) %all-to-all-start) | async-done | bytes 524320 | tf_op jit(solution)/shard_map/all_to_all | solution.py:34
  49.0 2.7 %collective-permute-start.3 = (bf16[64,4096]{1,0:T(8,128)(2,1)}, bf16[64,4096]{1,0:T(8,128)(2,1)}, u32[]{:S(2)}, u32[]{:S(2)}) collective-permute-start(bf16[64,4096]{1,0:T(8,128)(2,1)} %bitcast), channel_id=1, source_target_pairs={{0,1},{1,0},{2,3},{3,2},{4,5},{5,4},{6,7},{7,6},{8,9},{9,8},{10,11... | collective-permute-start | bytes 1572872 | tf_op jit(solution)/shard_map/ppermute | solution.py:24
  51.7 13.4 %all_to_all.31 = bf16[8,8,512]{2,1,0:T(8,128)(2,1)S(1)} all-to-all(bf16[8,8,512]{2,1,0:T(8,128)(2,1)S(1)} %bitcast.41), channel_id=1, replica_groups=mesh['ylo'=4,'z'=8,'x'=4,'yhi'=2,'core'=2] {'z'}, dimensions={0} | all-to-all | bytes 131072 | tf_op jit(solution)/shard_map/all_to_all | solution.py:51
  65.1 7.8 %collective-permute-start.9 = (bf16[64,512]{1,0:T(8,128)(2,1)S(1)}, bf16[64,512]{1,0:T(8,128)(2,1)S(1)}, u32[]{:S(2)}, u32[]{:S(2)}) collective-permute-start(bf16[64,512]{1,0:T(8,128)(2,1)S(1)} %bitcast.44), channel_id=1, source_target_pairs={{0,2},{2,0},{1,3},{3,1},{4,6},{6,4},{5,7},{7,5},{8,10},{10,8},{9,1... | collective-permute-start | bytes 196616 | tf_op jit(solution)/shard_map/ppermute | solution.py:24
  73.0 1.6 %collective-permute-done.9 = bf16[64,512]{1,0:T(8,128)(2,1)S(1)} collective-permute-done((bf16[64,512]{1,0:T(8,128)(2,1)S(1)}, bf16[64,512]{1,0:T(8,128)(2,1)S(1)}, u32[]{:S(2)}, u32[]{:S(2)}) %collective-permute-start.9) | collective-permute-done | bytes 65568 | tf_op jit(solution)/shard_map/ppermute | solution.py:24
  74.6 1.5 broadcast_in_dim.5
  76.1 4.5 %all-to-all-start.1 = ((bf16[8,128,896]{2,1,0:T(8,128)(2,1)}), bf16[8,128,896]{2,1,0:T(8,128)(2,1)}, u32[]{:S(2)}, u32[]{:S(2)}) async-start(bf16[8,128,896]{2,1,0:T(8,128)(2,1)} %broadcast_in_dim.5), calls=%async_computation.1 | async-start | bytes 3670016 | tf_op jit(solution)/shard_map/all_to_all | solution.py:34
  80.5 12.1 %all_gather.7 = bf16[512,512]{1,0:T(8,128)(2,1)} all-gather(bf16[128,512]{1,0:T(8,128)(2,1)S(1)} %pad_maximum_fusion.4), channel_id=1, replica_groups=mesh['ylo'=4,'z'=8,'x'=4,'yhi'=2,'core'=2] {'x'}, dimensions={0}, use_global_device_ids=true | all-gather | bytes 655360 | tf_op jit(solution)/shard_map/all_gather | solution.py:77
  92.6 6.2 %collective-permute-start.10 = (bf16[512,512]{1,0:T(8,128)(2,1)}, bf16[512,512]{1,0:T(8,128)(2,1)}, u32[]{:S(2)}, u32[]{:S(2)}) collective-permute-start(bf16[512,512]{1,0:T(8,128)(2,1)} %all_gather.7), channel_id=1, source_target_pairs={{0,1},{1,0},{2,3},{3,2},{4,5},{5,4},{6,7},{7,6},{8,9},{9,8},{10,11... | collective-permute-start | bytes 1572872 | tf_op jit(solution)/shard_map/ppermute | solution.py:24
  98.9 6.0 %fusion.5 = f32[128,896]{1,0:T(8,128)S(1)} fusion(bf16[896,4096]{1,0:T(8,128)(2,1)} %param.9, bf16[64,4096]{1,0:T(8,128)(2,1)} %collective-permute-done.3, bf16[64,4096]{1,0:T(8,128)(2,1)} %bitcast), kind=kOutput, calls=%fused_computation.12 | convolution fusion | flops 941850624 | bytes 8847360 | tf_op jit(solution)/shard_map/dot_general | solution.py:18
  104.9 2.4 %fusion.14 = f32[128,4096]{1,0:T(8,128)S(1)} fusion(bf16[4096,896]{1,0:T(8,128)(2,1)S(1)} %bitcast.31, f32[128,896]{1,0:T(8,128)S(1)} %copy-done.1, f32[128,896]{1,0:T(8,128)S(1)} %fusion.5, f32[128,896]{1,0:T(8,128)S(1)} %copy-done.2), kind=kOutput, calls=%fused_computation.29 | convolution fusion | flops 940670976 | bytes 10813440 | tf_op jit(solution)/shard_map/dot_general | solution.py:18
  107.4 2.5 %fusion = bf16[128,4096]{1,0:T(8,128)(2,1)S(1)} fusion(f32[128,4096]{1,0:T(8,128)S(1)} %fusion.14, bf16[4096,896]{1,0:T(8,128)(2,1)S(1)} %bitcast.35, f32[128,896]{1,0:T(8,128)S(1)} %fusion.5, f32[128,896]{1,0:T(8,128)S(1)} %copy-done.1), kind=kOutput, calls=%fused_computation.1 | convolution fusion | flops 941260800 | bytes 11403264 | tf_op jit(solution)/shard_map/dot_general | solution.py:18
  109.9 1.9 %collective-permute-start.4 = (bf16[64,4096]{1,0:T(8,128)(2,1)S(1)}, bf16[64,4096]{1,0:T(8,128)(2,1)S(1)}, u32[]{:S(2)}, u32[]{:S(2)}) collective-permute-start(bf16[64,4096]{1,0:T(8,128)(2,1)S(1)} %slice.34), channel_id=1, source_target_pairs={{0,1},{1,0},{2,3},{3,2},{4,5},{5,4},{6,7},{7,6},{8,9},{9,8},{10,11... | collective-permute-start | bytes 1572872 | tf_op jit(solution)/shard_map/ppermute | solution.py:24
  113.9 3.3 %collective-permute-start.7 = (bf16[16,4096]{1,0:T(8,128)(2,1)S(1)}, bf16[16,4096]{1,0:T(8,128)(2,1)S(1)}, u32[]{:S(2)}, u32[]{:S(2)}) collective-permute-start(bf16[16,4096]{1,0:T(8,128)(2,1)S(1)} %get-tuple-element.11), channel_id=1, source_target_pairs={{0,12},{4,0},{8,4},{12,8},{1,13},{5,1},{9,5},{13,9},{2,14},{6,2},{... | collective-permute-start | bytes 393224 | tf_op jit(solution)/shard_map/ppermute | solution.py:93
  117.2 2.5 %collective-permute-start.6 = (bf16[16,4096]{1,0:T(8,128)(2,1)S(1)}, bf16[16,4096]{1,0:T(8,128)(2,1)S(1)}, u32[]{:S(2)}, u32[]{:S(2)}) collective-permute-start(bf16[16,4096]{1,0:T(8,128)(2,1)S(1)} %get-tuple-element.12), channel_id=1, source_target_pairs={{0,8},{4,12},{8,0},{12,4},{1,9},{5,13},{9,1},{13,5},{2,10},{6,14},... | collective-permute-start | bytes 393224 | tf_op jit(solution)/shard_map/ppermute | solution.py:93
  119.7 2.2 %collective-permute-start.5 = (bf16[16,4096]{1,0:T(8,128)(2,1)S(1)}, bf16[16,4096]{1,0:T(8,128)(2,1)S(1)}, u32[]{:S(2)}, u32[]{:S(2)}) collective-permute-start(bf16[16,4096]{1,0:T(8,128)(2,1)S(1)} %get-tuple-element.10), channel_id=1, source_target_pairs={{0,4},{4,8},{8,12},{12,0},{1,5},{5,9},{9,13},{13,1},{2,6},{6,10},{... | collective-permute-start | bytes 393224 | tf_op jit(solution)/shard_map/ppermute | solution.py:93
  121.9 2.1 %all-to-all-done.1 = bf16[8,128,896]{2,1,0:T(8,128)(2,1)} async-done(((bf16[8,128,896]{2,1,0:T(8,128)(2,1)}), bf16[8,128,896]{2,1,0:T(8,128)(2,1)}, u32[]{:S(2)}, u32[]{:S(2)}) %all-to-all-start.1) | async-done | bytes 1835040 | tf_op jit(solution)/shard_map/all_to_all | solution.py:34
  124.0 2.2 %fusion.4 = bf16[896,128]{1,0:T(8,128)(2,1)S(1)} fusion(bf16[1024,896]{1,0:T(8,128)(2,1)} %bitcast.1, bf16[1024,512]{1,0:T(8,128)(2,1)S(1)} %bitcast.37), kind=kOutput, calls=%fused_computation.10 | convolution fusion | flops 235110400 | bytes 2326528 | tf_op jit(solution)/shard_map/dot_general | solution.py:12
  126.2 2.2 %fusion.3 = bf16[896,128]{1,0:T(8,128)(2,1)S(1)} fusion(bf16[1024,896]{1,0:T(8,128)(2,1)} %bitcast.1, bf16[1024,512]{1,0:T(8,128)(2,1)S(1)} %bitcast.38), kind=kOutput, calls=%fused_computation.9 | convolution fusion | flops 235110400 | bytes 2326528 | tf_op jit(solution)/shard_map/dot_general | solution.py:12
  128.4 2.2 %fusion.2 = bf16[896,128]{1,0:T(8,128)(2,1)S(1)} fusion(bf16[1024,896]{1,0:T(8,128)(2,1)} %bitcast.1, bf16[1024,512]{1,0:T(8,128)(2,1)S(1)} %bitcast.39), kind=kOutput, calls=%fused_computation.8 | convolution fusion | flops 235110400 | bytes 2326528 | tf_op jit(solution)/shard_map/dot_general | solution.py:12
  130.6 2.2 %fusion.1 = bf16[896,128]{1,0:T(8,128)(2,1)S(1)} fusion(bf16[1024,896]{1,0:T(8,128)(2,1)} %bitcast.1, bf16[1024,512]{1,0:T(8,128)(2,1)S(1)} %bitcast.40), kind=kOutput, calls=%fused_computation.7 | convolution fusion | flops 235110400 | bytes 2326528 | tf_op jit(solution)/shard_map/dot_general | solution.py:12
  133.8 3.5 %all-to-all-start.3 = ((bf16[4,896,128]{2,1,0:T(8,128)(2,1)}), bf16[4,896,128]{2,1,0:T(8,128)(2,1)S(1)}, u32[]{:S(2)}, u32[]{:S(2)}) async-start(bf16[4,896,128]{2,1,0:T(8,128)(2,1)} %bitcast.8), calls=%async_computation.3 | async-start | bytes 1835008 | tf_op jit(solution)/shard_map/all_to_all | solution.py:86
  137.4 7.7 %collective-permute-start.8 = (bf16[8,4096]{1,0:T(8,128)(2,1)S(1)}, bf16[8,4096]{1,0:T(8,128)(2,1)S(1)}, u32[]{:S(2)}, u32[]{:S(2)}) collective-permute-start(bf16[8,4096]{1,0:T(8,128)(2,1)S(1)} %slice.54), channel_id=1, source_target_pairs={{0,2},{2,0},{1,3},{3,1},{4,6},{6,4},{5,7},{7,5},{8,10},{10,8},{9,1... | collective-permute-start | bytes 196616 | tf_op jit(solution)/shard_map/ppermute | solution.py:24
  145.2 13.8 %collective-permute-done.8 = bf16[8,4096]{1,0:T(8,128)(2,1)S(1)} collective-permute-done((bf16[8,4096]{1,0:T(8,128)(2,1)S(1)}, bf16[8,4096]{1,0:T(8,128)(2,1)S(1)}, u32[]{:S(2)}, u32[]{:S(2)}) %collective-permute-start.8) | collective-permute-done | bytes 65568 | tf_op jit(solution)/shard_map/ppermute | solution.py:24
  159.6 2.9 %all-to-all-done.3 = bf16[4,896,128]{2,1,0:T(8,128)(2,1)S(1)} async-done(((bf16[4,896,128]{2,1,0:T(8,128)(2,1)}), bf16[4,896,128]{2,1,0:T(8,128)(2,1)S(1)}, u32[]{:S(2)}, u32[]{:S(2)}) %all-to-all-start.3) | async-done | bytes 917536 | tf_op jit(solution)/shard_map/all_to_all | solution.py:86
  (50 shorter events, 8.1 us)
Async XLA Ops:
  0.6 10.2 %collective-permute-start.1 = (bf16[8,4096]{1,0:T(8,128)(2,1)}, bf16[8,4096]{1,0:T(8,128)(2,1)S(1)}, u32[]{:S(2)}, u32[]{:S(2)}) collective-permute-start(bf16[8,4096]{1,0:T(8,128)(2,1)} %param.5), channel_id=1, source_target_pairs={{0,2},{2,0},{1,3},{3,1},{4,6},{6,4},{5,7},{7,5},{8,10},{10,8},{9,1... | collective-permute-start | bytes 196616 | tf_op jit(solution)/shard_map/ppermute | solution.py:24
  8.9 24.5 %collective-permute-start = (bf16[8,4096]{1,0:T(8,128)(2,1)}, bf16[8,4096]{1,0:T(8,128)(2,1)S(1)}, u32[]{:S(2)}, u32[]{:S(2)}) collective-permute-start(bf16[8,4096]{1,0:T(8,128)(2,1)} %param.6), channel_id=1, source_target_pairs={{0,2},{2,0},{1,3},{3,1},{4,6},{6,4},{5,7},{7,5},{8,10},{10,8},{9,1... | collective-permute-start | bytes 196616 | tf_op jit(solution)/shard_map/ppermute | solution.py:24
  22.5 16.8 %collective-permute-start.2 = (bf16[64,4096]{1,0:T(8,128)(2,1)S(1)}, bf16[64,4096]{1,0:T(8,128)(2,1)S(1)}, u32[]{:S(2)}, u32[]{:S(2)}) collective-permute-start(bf16[64,4096]{1,0:T(8,128)(2,1)S(1)} %all_gather.6), channel_id=1, source_target_pairs={{0,1},{1,0},{2,3},{3,2},{4,5},{5,4},{6,7},{7,6},{8,9},{9,8},{10,11... | collective-permute-start | bytes 1572872 | tf_op jit(solution)/shard_map/ppermute | solution.py:24
  35.1 13.8 %all-to-all-start = ((bf16[4,16,4096]{2,1,0:T(8,128)(2,1)}), bf16[4,16,4096]{2,1,0:T(8,128)(2,1)}, u32[]{:S(2)}, u32[]{:S(2)}) async-start(bf16[4,16,4096]{2,1,0:T(8,128)(2,1)} %broadcast_in_dim.4), calls=%async_computation | async-start | bytes 1048576 | tf_op jit(solution)/shard_map/all_to_all | solution.py:34
  39.3 5.4 %slice-start.2 = ((s8[7340032]{0:T(1024)(128)(4,1)}), s8[4194304]{0:T(1024)(128)(4,1)S(1)}, s32[]{:S(2)}) async-start(s8[7340032]{0:T(1024)(128)(4,1)} %bitcast.32), calls=%async_computation.6 | async-start | bytes 8388608
  39.4 5.3 %slice-start.3 = ((s8[7340032]{0:T(1024)(128)(4,1)}), s8[3145728]{0:T(1024)(128)(4,1)S(1)}, s32[]{:S(2)}) async-start(s8[7340032]{0:T(1024)(128)(4,1)} %bitcast.32), calls=%async_computation.7 | async-start | bytes 6291456
  43.9 0.8 copy-start
  44.7 7.0 %copy-start.3 = (bf16[8,4096]{1,0:T(8,128)(2,1)S(1)}, bf16[8,4096]{1,0:T(8,128)(2,1)}, u32[]{:S(2)}) copy-start(bf16[8,4096]{1,0:T(8,128)(2,1)} %param.6) | copy-start | bytes 196612
  49.0 49.9 %collective-permute-start.3 = (bf16[64,4096]{1,0:T(8,128)(2,1)}, bf16[64,4096]{1,0:T(8,128)(2,1)}, u32[]{:S(2)}, u32[]{:S(2)}) collective-permute-start(bf16[64,4096]{1,0:T(8,128)(2,1)} %bitcast), channel_id=1, source_target_pairs={{0,1},{1,0},{2,3},{3,2},{4,5},{5,4},{6,7},{7,6},{8,9},{9,8},{10,11... | collective-permute-start | bytes 1572872 | tf_op jit(solution)/shard_map/ppermute | solution.py:24
  65.1 9.4 %collective-permute-start.9 = (bf16[64,512]{1,0:T(8,128)(2,1)S(1)}, bf16[64,512]{1,0:T(8,128)(2,1)S(1)}, u32[]{:S(2)}, u32[]{:S(2)}) collective-permute-start(bf16[64,512]{1,0:T(8,128)(2,1)S(1)} %bitcast.44), channel_id=1, source_target_pairs={{0,2},{2,0},{1,3},{3,1},{4,6},{6,4},{5,7},{7,5},{8,10},{10,8},{9,1... | collective-permute-start | bytes 196616 | tf_op jit(solution)/shard_map/ppermute | solution.py:24
  74.6 30.3 %slice-start = ((s8[7340032]{0:T(1024)(128)(4,1)}), s8[3145728]{0:T(1024)(128)(4,1)S(1)}, s32[]{:S(2)}) async-start(s8[7340032]{0:T(1024)(128)(4,1)} %bitcast.30), calls=%async_computation.4 | async-start | bytes 6291456
  76.1 47.9 %all-to-all-start.1 = ((bf16[8,128,896]{2,1,0:T(8,128)(2,1)}), bf16[8,128,896]{2,1,0:T(8,128)(2,1)}, u32[]{:S(2)}, u32[]{:S(2)}) async-start(bf16[8,128,896]{2,1,0:T(8,128)(2,1)} %broadcast_in_dim.5), calls=%async_computation.1 | async-start | bytes 3670016 | tf_op jit(solution)/shard_map/all_to_all | solution.py:34
  92.6 12.3 %slice-start.1 = ((s8[7340032]{0:T(1024)(128)(4,1)}), s8[4194304]{0:T(1024)(128)(4,1)S(1)}, s32[]{:S(2)}) async-start(s8[7340032]{0:T(1024)(128)(4,1)} %bitcast.30), calls=%async_computation.5 | async-start | bytes 8388608
  92.6 12.3 %copy-start.1 = (f32[128,896]{1,0:T(8,128)S(1)}, f32[128,896]{1,0:T(8,128)}, u32[]{:S(2)}) copy-start(f32[128,896]{1,0:T(8,128)} %copy-done) | copy-start | bytes 1376260
  92.6 12.3 %copy-start.2 = (f32[128,896]{1,0:T(8,128)S(1)}, f32[128,896]{1,0:T(8,128)}, u32[]{:S(2)}) copy-start(f32[128,896]{1,0:T(8,128)} %get-tuple-element.14) | copy-start | bytes 1376260
  92.6 19.3 %collective-permute-start.10 = (bf16[512,512]{1,0:T(8,128)(2,1)}, bf16[512,512]{1,0:T(8,128)(2,1)}, u32[]{:S(2)}, u32[]{:S(2)}) collective-permute-start(bf16[512,512]{1,0:T(8,128)(2,1)} %all_gather.7), channel_id=1, source_target_pairs={{0,1},{1,0},{2,3},{3,2},{4,5},{5,4},{6,7},{7,6},{8,9},{9,8},{10,11... | collective-permute-start | bytes 1572872 | tf_op jit(solution)/shard_map/ppermute | solution.py:24
  98.9 8.5 %slice-start.4 = ((s8[7340032]{0:T(1024)(128)(4,1)}), s8[4194304]{0:T(1024)(128)(4,1)S(1)}, s32[]{:S(2)}) async-start(s8[7340032]{0:T(1024)(128)(4,1)} %bitcast.34), calls=%async_computation.8 | async-start | bytes 8388608
  104.9 2.5 %slice-start.5 = ((s8[7340032]{0:T(1024)(128)(4,1)}), s8[3145728]{0:T(1024)(128)(4,1)S(1)}, s32[]{:S(2)}) async-start(s8[7340032]{0:T(1024)(128)(4,1)} %bitcast.34), calls=%async_computation.9 | async-start | bytes 6291456
  109.9 3.8 %collective-permute-start.4 = (bf16[64,4096]{1,0:T(8,128)(2,1)S(1)}, bf16[64,4096]{1,0:T(8,128)(2,1)S(1)}, u32[]{:S(2)}, u32[]{:S(2)}) collective-permute-start(bf16[64,4096]{1,0:T(8,128)(2,1)S(1)} %slice.34), channel_id=1, source_target_pairs={{0,1},{1,0},{2,3},{3,2},{4,5},{5,4},{6,7},{7,6},{8,9},{9,8},{10,11... | collective-permute-start | bytes 1572872 | tf_op jit(solution)/shard_map/ppermute | solution.py:24
  113.9 23.4 %collective-permute-start.7 = (bf16[16,4096]{1,0:T(8,128)(2,1)S(1)}, bf16[16,4096]{1,0:T(8,128)(2,1)S(1)}, u32[]{:S(2)}, u32[]{:S(2)}) collective-permute-start(bf16[16,4096]{1,0:T(8,128)(2,1)S(1)} %get-tuple-element.11), channel_id=1, source_target_pairs={{0,12},{4,0},{8,4},{12,8},{1,13},{5,1},{9,5},{13,9},{2,14},{6,2},{... | collective-permute-start | bytes 393224 | tf_op jit(solution)/shard_map/ppermute | solution.py:93
  117.2 20.1 %collective-permute-start.6 = (bf16[16,4096]{1,0:T(8,128)(2,1)S(1)}, bf16[16,4096]{1,0:T(8,128)(2,1)S(1)}, u32[]{:S(2)}, u32[]{:S(2)}) collective-permute-start(bf16[16,4096]{1,0:T(8,128)(2,1)S(1)} %get-tuple-element.12), channel_id=1, source_target_pairs={{0,8},{4,12},{8,0},{12,4},{1,9},{5,13},{9,1},{13,5},{2,10},{6,14},... | collective-permute-start | bytes 393224 | tf_op jit(solution)/shard_map/ppermute | solution.py:93
  119.7 17.7 %collective-permute-start.5 = (bf16[16,4096]{1,0:T(8,128)(2,1)S(1)}, bf16[16,4096]{1,0:T(8,128)(2,1)S(1)}, u32[]{:S(2)}, u32[]{:S(2)}) collective-permute-start(bf16[16,4096]{1,0:T(8,128)(2,1)S(1)} %get-tuple-element.10), channel_id=1, source_target_pairs={{0,4},{4,8},{8,12},{12,0},{1,5},{5,9},{9,13},{13,1},{2,6},{6,10},{... | collective-permute-start | bytes 393224 | tf_op jit(solution)/shard_map/ppermute | solution.py:93
  133.8 28.6 %all-to-all-start.3 = ((bf16[4,896,128]{2,1,0:T(8,128)(2,1)}), bf16[4,896,128]{2,1,0:T(8,128)(2,1)S(1)}, u32[]{:S(2)}, u32[]{:S(2)}) async-start(bf16[4,896,128]{2,1,0:T(8,128)(2,1)} %bitcast.8), calls=%async_computation.3 | async-start | bytes 1835008 | tf_op jit(solution)/shard_map/all_to_all | solution.py:86
  137.4 21.5 %collective-permute-start.8 = (bf16[8,4096]{1,0:T(8,128)(2,1)S(1)}, bf16[8,4096]{1,0:T(8,128)(2,1)S(1)}, u32[]{:S(2)}, u32[]{:S(2)}) collective-permute-start(bf16[8,4096]{1,0:T(8,128)(2,1)S(1)} %slice.54), channel_id=1, source_target_pairs={{0,2},{2,0},{1,3},{3,1},{4,6},{6,4},{5,7},{7,5},{8,10},{10,8},{9,1... | collective-permute-start | bytes 196616 | tf_op jit(solution)/shard_map/ppermute | solution.py:24

commit v2 on v1

v2 whole, which is shorter than its diff:
```python
import jax
import jax.numpy as jnp
from jax import lax
from jax.sharding import Mesh, PartitionSpec as P

SIZES = (4, 8, 4, 2, 2)
NAMES = ("ylo", "z", "x", "yhi", "core")
SWAP = [(0, 1), (1, 0)]


def contract_rows(left, right):
    return lax.dot_general(
        left, right, (((0,), (0,)), ((), ())), preferred_element_type=jnp.float32
    )


def contract_cols(left, right):
    return lax.dot_general(
        left, right, (((1,), (1,)), ((), ())), preferred_element_type=jnp.float32
    )


def swap(value, axis):
    return lax.ppermute(value, axis, SWAP)


def both(rows, axis):
    return jnp.concatenate([rows, swap(rows, axis)], axis=0)


def gather_a2a(value, axis):
    copies = jnp.broadcast_to(value, (lax.axis_size(axis),) + value.shape[1:])
    return lax.all_to_all(copies, axis, 0, 0)


def after(value, *earlier):
    return lax.optimization_barrier((value,) + earlier)[0]


def in_order(own, other, index):
    first, second = jnp.where(index == 0, own, other), jnp.where(index == 0, other, own)
    return jnp.concatenate([first, second], axis=0)


def body(tokens, upstream_grad, w_gate, w_up, w_down):
    rows, width = tokens.shape
    f_dev = w_gate.shape[1]
    n_y, n_z, n_x = lax.axis_size("ylo"), lax.axis_size("z"), lax.axis_size("x")
    block = width // (n_y * n_z)

    cols = upstream_grad.reshape(rows, n_y, n_z * block).transpose(1, 0, 2)
    me_h = lax.axis_index("yhi")
    cols = jnp.broadcast_to(cols[:, None], (n_y, 2, rows, n_z * block))
    cols = lax.all_to_all(cols.reshape(2 * n_y, rows, -1), ("ylo", "yhi"), 0, 0)
    cols = cols.reshape(n_y, 2, rows, n_z * block).transpose(1, 2, 0, 3).reshape(2 * rows, width)

    other = swap(jnp.concatenate([tokens, upstream_grad], axis=0), "yhi")
    tokens2 = in_order(tokens, other[:rows], me_h)
    upstream2 = in_order(upstream_grad, other[rows:], me_h)
    pair = jnp.stack([upstream2, cols], axis=0)[None]

    tokens_x = lax.all_gather(tokens2, "x", axis=0, tiled=True)
    gathered = both(tokens_x, "core")
    pair_x = gather_a2a(after(pair, tokens_x), "x")
    gate_pre = jnp.dot(gathered, w_gate, preferred_element_type=jnp.float32)
    up_pre = jnp.dot(gathered, w_up, preferred_element_type=jnp.float32)
    sig_gate = jax.nn.sigmoid(gate_pre)
    act_gate = gate_pre * sig_gate
    hidden = (act_gate * up_pre).astype(jnp.bfloat16)

    hidden_y = lax.all_gather(hidden, "ylo", axis=0)
    pair_x = after(pair_x, hidden_y)
    cols = both(pair_x[:, 1].reshape(-1, width), "core").reshape(-1, n_y, n_z * block)
    factor = float(n_z * cols.shape[0] * n_y) ** (-0.5)
    down = lax.dot_general(
        hidden_y, cols, (((0, 1), (1, 0)), ((), ())), preferred_element_type=jnp.float32
    )
    down = (down * factor).astype(jnp.bfloat16).reshape(f_dev, n_z, block).transpose(1, 0, 2)
    down_z = lax.all_to_all(down, "z", 0, 0)

    upstream = both(after(pair_x, down)[:, 0].reshape(-1, width), "core")
    grad_hidden = contract_cols(upstream, w_down).astype(jnp.bfloat16)
    hidden_f = grad_hidden.astype(jnp.float32)
    grad_gate = (hidden_f * up_pre * sig_gate * (1.0 + gate_pre * (1.0 - sig_gate))).astype(
        jnp.bfloat16
    )
    grad_up = (hidden_f * act_gate).astype(jnp.bfloat16)
    partial = (contract_cols(grad_gate, w_gate) + contract_cols(grad_up, w_up)).astype(jnp.bfloat16)

    half = partial.shape[0] // 2
    other = []
    for k in range(2):
        cut = partial[half:, k * width // 2 : (k + 1) * width // 2]
        cut = lax.all_gather(cut, "core", axis=0)
        other.append(lax.dynamic_index_in_dim(cut, 1 - lax.axis_index("core"), 0, keepdims=False))
    other = jnp.concatenate(other, axis=1)
    partial = (partial[:half].astype(jnp.float32) + other.astype(jnp.float32)).astype(jnp.bfloat16)
    me = lax.axis_index("x")
    chunk = 2 * rows
    total = lax.dynamic_slice_in_dim(partial, me * chunk, chunk, 0).astype(jnp.float32)
    for k in range(1, n_x):
        piece = lax.dynamic_slice_in_dim(partial, lax.rem(me + k, n_x) * chunk, chunk, 0)
        piece = lax.ppermute(piece, "x", [(i, (i + k) % n_x) for i in range(n_x)])
        total = total + piece.astype(jnp.float32)
    total = total.reshape(2, rows, width)
    mine = lax.dynamic_index_in_dim(total, me_h, 0, keepdims=False)
    sent = lax.dynamic_index_in_dim(total, 1 - me_h, 0, keepdims=False).astype(jnp.bfloat16)
    sent = lax.all_gather(sent, "yhi", axis=0)
    other = lax.dynamic_index_in_dim(sent, 1 - me_h, 0, keepdims=False)
    summed = (mine + other.astype(jnp.float32)).astype(jnp.bfloat16)

    grad_down = down_z.astype(jnp.float32).sum(0)
    return (summed, grad_down)


def solution(mesh):
    cut = Mesh(mesh.devices.reshape(SIZES), NAMES)
    dp, tensor = NAMES[:2], NAMES[2:]
    in_specs = (
        P(dp + tensor, None),
        P(dp + tensor, None),
        P(None, tensor),
        P(None, tensor),
        P(tensor, None),
    )
    out_specs = (P(dp + tensor, None), P(tensor, dp))
    return jax.shard_map(body, mesh=cut, in_specs=in_specs, out_specs=out_specs, check_vma=False)
```

time: 166 us -> 136 us (0.82)
  the two profiles are of different devices: /device:TPU:1 before, /device:TPU:2 now
where the time goes in v2:
time: 136 us; the launch traced here: 135 us
  blocking collectives  48.4 us (36%)
  starting transfers between devices  41.7 us (31%)
  matrix products  18.7 us (14%)
  waiting for transfers between devices  12.4 us (9%)
  local copies, waits for them, and re-layouts  7.97 us (6%)
  other arithmetic  5.22 us (4%)
    all_gather x1, blocking collectives, body(): hidden_y = lax.all_gather(hidden, 'ylo', axis=0)  20.3 us
    all_gather x1, blocking collectives, body(): tokens_x = lax.all_gather(tokens2, 'x', axis=0, tiled=True)  14.9 us
    ppermute x4, starting transfers between devices, swap(): return lax.ppermute(value, axis, SWAP)  13.6 us
    dot_general x3, matrix products, contract_cols(): lax.dot_general(left, right, (((1,), (1,)), ((), ())), preferred_element_...  10.9 us
    ppermute x3, starting transfers between devices, body(): piece = lax.ppermute(piece, 'x', [(i, (i + k) % n_x) for i in range(n_x)])  9.84 us
    all_gather x1, blocking collectives, body(): sent = lax.all_gather(sent, 'yhi', axis=0)  8.86 us
    all_to_all x1, starting transfers between devices, body(): down_z = lax.all_to_all(down, 'z', 0, 0)  8.13 us
    all_to_all x1, starting transfers between devices, gather_a2a(): return lax.all_to_all(copies, axis, 0, 0)  6.8 us
  transfers between devices with their start and end apart: 10, of which 4 were waited for; matrix products, arithmetic and copies ran while one was open for 17% of the time, Pallas kernels for 0%

profile of v2, /device:TPU:2, one launch (start us, length us, event | category | flops | bytes accessed | tf_op | source)
XLA Modules:
  0.0 135.4 jit_solution(7066550034236053350)
XLA Ops:
  0.6 0.9 pad_maximum_fusion
  1.5 7.7 %collective-permute-start = (bf16[16,4096]{1,0:T(8,128)(2,1)S(1)}, bf16[16,4096]{1,0:T(8,128)(2,1)S(1)}, u32[]{:S(2)}, u32[]{:S(2)}) collective-permute-start(bf16[16,4096]{1,0:T(8,128)(2,1)S(1)} %pad_maximum_fusion), channel_id=1, source_target_pairs={{0,2},{2,0},{1,3},{3,1},{4,6},{6,4},{5,7},{7,5},{8,10},{10,8},{9,1... | collective-permute-start | bytes 393224 | tf_op jit(solution)/shard_map/ppermute | solution.py:24
  9.3 1.5 %broadcast_in_dim.16 = bf16[4,2,8,1024]{3,2,1,0:T(8,128)(2,1)} broadcast(bf16[4,8,1024]{2,1,0:T(8,128)(2,1)} %bitcast.65), dimensions={0,2,3} | broadcast | bytes 196608 | tf_op jit(solution)/shard_map/broadcast_in_dim | solution.py:53
  10.8 3.4 %all-to-all-start = ((bf16[8,8,1024]{2,1,0:T(8,128)(2,1)}), bf16[8,8,1024]{2,1,0:T(8,128)(2,1)S(1)}, u32[]{:S(2)}, u32[]{:S(2)}) async-start(bf16[8,8,1024]{2,1,0:T(8,128)(2,1)} %bitcast.3), calls=%async_computation | async-start | bytes 262144 | tf_op jit(solution)/shard_map/all_to_all | solution.py:54
  14.2 0.9 broadcast_select_fusion.3
  15.1 14.9 %all_gather.25 = bf16[64,4096]{1,0:T(8,128)(2,1)S(1)} all-gather(bf16[16,4096]{1,0:T(8,128)(2,1)S(1)} %pad_maximum_fusion.1), channel_id=1, replica_groups=mesh['ylo'=4,'z'=8,'x'=4,'yhi'=2,'core'=2] {'x'}, dimensions={0}, use_global_device_ids=true | all-gather | bytes 655360 | tf_op jit(solution)/shard_map/all_gather | solution.py:62
  29.9 1.9 %collective-permute-start.1 = (bf16[64,4096]{1,0:T(8,128)(2,1)S(1)}, bf16[64,4096]{1,0:T(8,128)(2,1)S(1)}, u32[]{:S(2)}, u32[]{:S(2)}) collective-permute-start(bf16[64,4096]{1,0:T(8,128)(2,1)S(1)} %all_gather.25), channel_id=1, source_target_pairs={{0,1},{1,0},{2,3},{3,2},{4,5},{5,4},{6,7},{7,6},{8,9},{9,8},{10,11... | collective-permute-start | bytes 1572872 | tf_op jit(solution)/shard_map/ppermute | solution.py:24
  32.2 1.1 broadcast_in_dim.19
  33.3 6.8 %all-to-all-start.1 = ((bf16[4,2,16,4096]{3,2,1,0:T(8,128)(2,1)}), bf16[4,2,16,4096]{3,2,1,0:T(8,128)(2,1)S(1)}, u32[]{:S(2)}, u32[]{:S(2)}) async-start(bf16[4,2,16,4096]{3,2,1,0:T(8,128)(2,1)} %broadcast_in_dim.19), calls=%async_computation.1 | async-start | bytes 2097152 | tf_op jit(solution)/shard_map/all_to_all | solution.py:33
  40.1 4.5 %fusion.20 = f32[128,896]{1,0:T(8,128)S(1)} fusion(bf16[128,4096]{1,0:T(8,128)(2,1)S(1)} %constant_dynamic-update-slice_fusion, bf16[4096,896]{1,0:T(8,128)(2,1)} %param.7), kind=kOutput, calls=%fused_computation.48 | convolution fusion | flops 939524096 | bytes 8847360 | tf_op jit(solution)/shard_map/dot_general | solution.py:65
  44.6 0.7 slice-done.3
  45.3 2.1 %multiply_convert_fusion.2 = (bf16[128,896]{1,0:T(8,128)(2,1)S(1)}, f32[128,896]{1,0:T(8,128)}) fusion(f32[128,896]{1,0:T(8,128)S(1)} %fusion.20, bf16[128,4096]{1,0:T(8,128)(2,1)S(1)} %constant_dynamic-update-slice_fusion, bf16[4096,896]{1,0:T(8,128)(2,1)S(1)} %bitcast.56), kind=kOutput, calls=%fused_computation.19 | convolution fusion | flops 940212224 | bytes 9535488 | tf_op jit(solution)/shard_map/dot_general | solution.py:66
  47.4 20.3 %all-gather = bf16[512,896]{1,0:T(8,128)(2,1)S(1)} all-gather(bf16[128,896]{1,0:T(8,128)(2,1)S(1)} %get-tuple-element.19), channel_id=2, replica_groups=mesh['ylo'=4,'z'=8,'x'=4,'yhi'=2,'core'=2] {'ylo'}, dimensions={0}, use_global_device_ids=true | all-gather | bytes 1146880 | tf_op jit(solution)/shard_map/all_gather | solution.py:71
  67.8 1.9 %collective-permute-start.2 = (bf16[64,4096]{1,0:T(8,128)(2,1)S(1)}, bf16[64,4096]{1,0:T(8,128)(2,1)S(1)}, u32[]{:S(2)}, u32[]{:S(2)}) collective-permute-start(bf16[64,4096]{1,0:T(8,128)(2,1)S(1)} %bitcast.60), channel_id=1, source_target_pairs={{0,1},{1,0},{2,3},{3,2},{4,5},{5,4},{6,7},{7,6},{8,9},{9,8},{10,11... | collective-permute-start | bytes 1572872 | tf_op jit(solution)/shard_map/ppermute | solution.py:24
  70.3 1.3 collective-permute-done.2
  71.6 1.2 fusion.2
  72.8 1.6 %copy.25 = bf16[112,8,8,128]{3,2,0,1:T(8,128)(2,1)} copy(bf16[112,8,8,128]{3,2,1,0:T(8,128)(2,1)S(1)} %fusion.2) | data formatting | bytes 3670016 | tf_op jit(solution)/shard_map/reshape | solution.py:78
  74.4 2.0 %slice.24 = bf16[4,1,16,4096]{3,2,1,0:T(8,128)(2,1)} slice(bf16[4,2,16,4096]{3,2,1,0:T(8,128)(2,1)} %copy-done.2), slice={[0:4], [0:1], [0:16], [0:4096]} | slice | bytes 1048576 | tf_op jit(solution)/shard_map/slice | solution.py:81
  76.4 2.0 %collective-permute-start.3 = (bf16[64,4096]{1,0:T(8,128)(2,1)}, bf16[64,4096]{1,0:T(8,128)(2,1)}, u32[]{:S(2)}, u32[]{:S(2)}) collective-permute-start(bf16[64,4096]{1,0:T(8,128)(2,1)} %bitcast.12), channel_id=1, source_target_pairs={{0,1},{1,0},{2,3},{3,2},{4,5},{5,4},{6,7},{7,6},{8,9},{9,8},{10,11... | collective-permute-start | bytes 1572872 | tf_op jit(solution)/shard_map/ppermute | solution.py:24
  78.5 8.1 %all-to-all-start.2 = ((bf16[8,896,128]{2,1,0:T(8,128)(2,1)}), bf16[8,896,128]{2,1,0:T(8,128)(2,1)}, u32[]{:S(2)}, u32[]{:S(2)}) async-start(bf16[8,896,128]{2,1,0:T(8,128)(2,1)} %bitcast.59), calls=%async_computation.2 | async-start | bytes 3670016 | tf_op jit(solution)/shard_map/all_to_all | solution.py:79
  86.7 6.0 %fusion.3 = f32[128,896]{1,0:T(8,128)S(1)} fusion(bf16[896,4096]{1,0:T(8,128)(2,1)} %param.9, bf16[64,4096]{1,0:T(8,128)(2,1)} %collective-permute-done.3, bf16[64,4096]{1,0:T(8,128)(2,1)} %bitcast.12), kind=kOutput, calls=%fused_computation.8 | convolution fusion | flops 941850624 | bytes 8847360 | tf_op jit(solution)/shard_map/dot_general | solution.py:18
  92.7 2.4 %fusion.11 = f32[128,4096]{1,0:T(8,128)S(1)} fusion(bf16[4096,896]{1,0:T(8,128)(2,1)S(1)} %bitcast.54, f32[128,896]{1,0:T(8,128)S(1)} %copy-done.1, f32[128,896]{1,0:T(8,128)S(1)} %fusion.3, f32[128,896]{1,0:T(8,128)S(1)} %copy-done.3), kind=kOutput, calls=%fused_computation.26 | convolution fusion | flops 940670976 | bytes 10813440 | tf_op jit(solution)/shard_map/dot_general | solution.py:18
  95.2 2.5 %fusion = bf16[128,4096]{1,0:T(8,128)(2,1)S(1)} fusion(f32[128,4096]{1,0:T(8,128)S(1)} %fusion.11, bf16[4096,896]{1,0:T(8,128)(2,1)S(1)} %bitcast.58, f32[128,896]{1,0:T(8,128)S(1)} %fusion.3, f32[128,896]{1,0:T(8,128)S(1)} %copy-done.1), kind=kOutput, calls=%fused_computation.1 | convolution fusion | flops 941260800 | bytes 11403264 | tf_op jit(solution)/shard_map/dot_general | solution.py:18
  97.7 2.2 %all-gather.1 = bf16[128,2048]{1,0:T(8,128)(2,1)S(1)} all-gather(bf16[64,2048]{1,0:T(8,128)(2,1)S(1)} %get-tuple-element.8), channel_id=3, replica_groups=mesh['ylo'=4,'z'=8,'x'=4,'yhi'=2,'core'=2] {'core'}, dimensions={0}, use_global_device_ids=true | all-gather | bytes 786432 | tf_op jit(solution)/shard_map/all_gather | solution.py:94
  99.9 2.2 %all-gather.2 = bf16[128,2048]{1,0:T(8,128)(2,1)S(1)} all-gather(bf16[64,2048]{1,0:T(8,128)(2,1)S(1)} %get-tuple-element.9), channel_id=4, replica_groups=mesh['ylo'=4,'z'=8,'x'=4,'yhi'=2,'core'=2] {'core'}, dimensions={0}, use_global_device_ids=true | all-gather | bytes 786432 | tf_op jit(solution)/shard_map/all_gather | solution.py:94
  102.3 3.4 %collective-permute-start.4 = (bf16[16,4096]{1,0:T(8,128)(2,1)S(1)}, bf16[16,4096]{1,0:T(8,128)(2,1)S(1)}, u32[]{:S(2)}, u32[]{:S(2)}) collective-permute-start(bf16[16,4096]{1,0:T(8,128)(2,1)S(1)} %get-tuple-element.10), channel_id=1, source_target_pairs={{0,4},{4,8},{8,12},{12,0},{1,5},{5,9},{9,13},{13,1},{2,6},{6,10},{... | collective-permute-start | bytes 393224 | tf_op jit(solution)/shard_map/ppermute | solution.py:103
  105.7 2.5 %collective-permute-start.6 = (bf16[16,4096]{1,0:T(8,128)(2,1)S(1)}, bf16[16,4096]{1,0:T(8,128)(2,1)S(1)}, u32[]{:S(2)}, u32[]{:S(2)}) collective-permute-start(bf16[16,4096]{1,0:T(8,128)(2,1)S(1)} %get-tuple-element.11), channel_id=1, source_target_pairs={{0,12},{4,0},{8,4},{12,8},{1,13},{5,1},{9,5},{13,9},{2,14},{6,2},{... | collective-permute-start | bytes 393224 | tf_op jit(solution)/shard_map/ppermute | solution.py:103
  108.2 4.0 %collective-permute-start.5 = (bf16[16,4096]{1,0:T(8,128)(2,1)S(1)}, bf16[16,4096]{1,0:T(8,128)(2,1)S(1)}, u32[]{:S(2)}, u32[]{:S(2)}) collective-permute-start(bf16[16,4096]{1,0:T(8,128)(2,1)S(1)} %get-tuple-element.12), channel_id=1, source_target_pairs={{0,8},{4,12},{8,0},{12,4},{1,9},{5,13},{9,1},{13,5},{2,10},{6,14},... | collective-permute-start | bytes 393224 | tf_op jit(solution)/shard_map/ppermute | solution.py:103
  112.9 3.7 %collective-permute-done.5 = bf16[16,4096]{1,0:T(8,128)(2,1)S(1)} collective-permute-done((bf16[16,4096]{1,0:T(8,128)(2,1)S(1)}, bf16[16,4096]{1,0:T(8,128)(2,1)S(1)}, u32[]{:S(2)}, u32[]{:S(2)}) %collective-permute-start.5) | collective-permute-done | bytes 131104 | tf_op jit(solution)/shard_map/ppermute | solution.py:103
  116.7 8.9 %all_gather.32 = bf16[2,8,4096]{2,1,0:T(8,128)(2,1)S(1)} all-gather(bf16[1,8,4096]{2,1,0:T(8,128)(2,1)S(1)} %dynamic-slice_convert_fusion), channel_id=1, replica_groups=mesh['ylo'=4,'z'=8,'x'=4,'yhi'=2,'core'=2] {'yhi'}, dimensions={0}, use_global_device_ids=true | all-gather | bytes 196608 | tf_op jit(solution)/shard_map/all_gather | solution.py:108
  126.2 6.7 %all-to-all-done.2 = bf16[8,896,128]{2,1,0:T(8,128)(2,1)} async-done(((bf16[8,896,128]{2,1,0:T(8,128)(2,1)}), bf16[8,896,128]{2,1,0:T(8,128)(2,1)}, u32[]{:S(2)}, u32[]{:S(2)}) %all-to-all-start.2) | async-done | bytes 1835040 | tf_op jit(solution)/shard_map/all_to_all | solution.py:79
  132.8 2.6 %convert_reduce_fusion = f32[896,128]{1,0:T(8,128)} fusion(bf16[8,896,128]{2,1,0:T(8,128)(2,1)} %all-to-all-done.2), kind=kLoop, calls=%fused_computation.4 | loop fusion | flops 1720320 | bytes 2293760 | tf_op jit(solution)/shard_map/reduce_sum | solution.py:112
  (48 shorter events, 2.6 us)
Async XLA Ops:
  1.5 12.6 %collective-permute-start = (bf16[16,4096]{1,0:T(8,128)(2,1)S(1)}, bf16[16,4096]{1,0:T(8,128)(2,1)S(1)}, u32[]{:S(2)}, u32[]{:S(2)}) collective-permute-start(bf16[16,4096]{1,0:T(8,128)(2,1)S(1)} %pad_maximum_fusion), channel_id=1, source_target_pairs={{0,2},{2,0},{1,3},{3,1},{4,6},{6,4},{5,7},{7,5},{8,10},{10,8},{9,1... | collective-permute-start | bytes 393224 | tf_op jit(solution)/shard_map/ppermute | solution.py:24
  10.8 21.2 %all-to-all-start = ((bf16[8,8,1024]{2,1,0:T(8,128)(2,1)}), bf16[8,8,1024]{2,1,0:T(8,128)(2,1)S(1)}, u32[]{:S(2)}, u32[]{:S(2)}) async-start(bf16[8,8,1024]{2,1,0:T(8,128)(2,1)} %bitcast.3), calls=%async_computation | async-start | bytes 262144 | tf_op jit(solution)/shard_map/all_to_all | solution.py:54
  29.9 10.1 %collective-permute-start.1 = (bf16[64,4096]{1,0:T(8,128)(2,1)S(1)}, bf16[64,4096]{1,0:T(8,128)(2,1)S(1)}, u32[]{:S(2)}, u32[]{:S(2)}) collective-permute-start(bf16[64,4096]{1,0:T(8,128)(2,1)S(1)} %all_gather.25), channel_id=1, source_target_pairs={{0,1},{1,0},{2,3},{3,2},{4,5},{5,4},{6,7},{7,6},{8,9},{9,8},{10,11... | collective-permute-start | bytes 1572872 | tf_op jit(solution)/shard_map/ppermute | solution.py:24
  33.3 34.5 %all-to-all-start.1 = ((bf16[4,2,16,4096]{3,2,1,0:T(8,128)(2,1)}), bf16[4,2,16,4096]{3,2,1,0:T(8,128)(2,1)S(1)}, u32[]{:S(2)}, u32[]{:S(2)}) async-start(bf16[4,2,16,4096]{3,2,1,0:T(8,128)(2,1)} %broadcast_in_dim.19), calls=%async_computation.1 | async-start | bytes 2097152 | tf_op jit(solution)/shard_map/all_to_all | solution.py:33
  40.1 4.6 %slice-start.2 = ((s8[7340032]{0:T(1024)(128)(4,1)}), s8[4194304]{0:T(1024)(128)(4,1)S(1)}, s32[]{:S(2)}) async-start(s8[7340032]{0:T(1024)(128)(4,1)} %bitcast.55), calls=%async_computation.5 | async-start | bytes 8388608
  40.1 5.2 %slice-start.3 = ((s8[7340032]{0:T(1024)(128)(4,1)}), s8[3145728]{0:T(1024)(128)(4,1)S(1)}, s32[]{:S(2)}) async-start(s8[7340032]{0:T(1024)(128)(4,1)} %bitcast.55), calls=%async_computation.6 | async-start | bytes 6291456
  45.3 2.1 %copy-start = (f32[128,896]{1,0:T(8,128)}, f32[128,896]{1,0:T(8,128)S(1)}, u32[]{:S(2)}) copy-start(f32[128,896]{1,0:T(8,128)S(1)} %fusion.20) | copy-start | bytes 1376260
  67.7 5.1 %copy-start.2 = (bf16[4,2,16,4096]{3,2,1,0:T(8,128)(2,1)}, bf16[4,2,16,4096]{3,2,1,0:T(8,128)(2,1)S(1)}, u32[]{:S(2)}) copy-start(bf16[4,2,16,4096]{3,2,1,0:T(8,128)(2,1)S(1)} %all-to-all-done.1) | copy-start | bytes 3145732
  67.8 3.8 %collective-permute-start.2 = (bf16[64,4096]{1,0:T(8,128)(2,1)S(1)}, bf16[64,4096]{1,0:T(8,128)(2,1)S(1)}, u32[]{:S(2)}, u32[]{:S(2)}) collective-permute-start(bf16[64,4096]{1,0:T(8,128)(2,1)S(1)} %bitcast.60), channel_id=1, source_target_pairs={{0,1},{1,0},{2,3},{3,2},{4,5},{5,4},{6,7},{7,6},{8,9},{9,8},{10,11... | collective-permute-start | bytes 1572872 | tf_op jit(solution)/shard_map/ppermute | solution.py:24
  74.4 18.3 %slice-start = ((s8[7340032]{0:T(1024)(128)(4,1)}), s8[3145728]{0:T(1024)(128)(4,1)S(1)}, s32[]{:S(2)}) async-start(s8[7340032]{0:T(1024)(128)(4,1)} %bitcast.53), calls=%async_computation.3 | async-start | bytes 6291456
  76.4 10.2 %collective-permute-start.3 = (bf16[64,4096]{1,0:T(8,128)(2,1)}, bf16[64,4096]{1,0:T(8,128)(2,1)}, u32[]{:S(2)}, u32[]{:S(2)}) collective-permute-start(bf16[64,4096]{1,0:T(8,128)(2,1)} %bitcast.12), channel_id=1, source_target_pairs={{0,1},{1,0},{2,3},{3,2},{4,5},{5,4},{6,7},{7,6},{8,9},{9,8},{10,11... | collective-permute-start | bytes 1572872 | tf_op jit(solution)/shard_map/ppermute | solution.py:24
  78.5 54.3 %all-to-all-start.2 = ((bf16[8,896,128]{2,1,0:T(8,128)(2,1)}), bf16[8,896,128]{2,1,0:T(8,128)(2,1)}, u32[]{:S(2)}, u32[]{:S(2)}) async-start(bf16[8,896,128]{2,1,0:T(8,128)(2,1)} %bitcast.59), calls=%async_computation.2 | async-start | bytes 3670016 | tf_op jit(solution)/shard_map/all_to_all | solution.py:79
  86.6 6.1 %slice-start.1 = ((s8[7340032]{0:T(1024)(128)(4,1)}), s8[4194304]{0:T(1024)(128)(4,1)S(1)}, s32[]{:S(2)}) async-start(s8[7340032]{0:T(1024)(128)(4,1)} %bitcast.53), calls=%async_computation.4 | async-start | bytes 8388608
  86.6 6.1 %copy-start.1 = (f32[128,896]{1,0:T(8,128)S(1)}, f32[128,896]{1,0:T(8,128)}, u32[]{:S(2)}) copy-start(f32[128,896]{1,0:T(8,128)} %copy-done) | copy-start | bytes 1376260
  86.6 6.1 %copy-start.3 = (f32[128,896]{1,0:T(8,128)S(1)}, f32[128,896]{1,0:T(8,128)}, u32[]{:S(2)}) copy-start(f32[128,896]{1,0:T(8,128)} %get-tuple-element.20) | copy-start | bytes 1376260
  86.7 8.5 %slice-start.4 = ((s8[7340032]{0:T(1024)(128)(4,1)}), s8[4194304]{0:T(1024)(128)(4,1)S(1)}, s32[]{:S(2)}) async-start(s8[7340032]{0:T(1024)(128)(4,1)} %bitcast.57), calls=%async_computation.7 | async-start | bytes 8388608
  92.7 2.5 %slice-start.5 = ((s8[7340032]{0:T(1024)(128)(4,1)}), s8[3145728]{0:T(1024)(128)(4,1)S(1)}, s32[]{:S(2)}) async-start(s8[7340032]{0:T(1024)(128)(4,1)} %bitcast.57), calls=%async_computation.8 | async-start | bytes 6291456
  102.3 9.9 %collective-permute-start.4 = (bf16[16,4096]{1,0:T(8,128)(2,1)S(1)}, bf16[16,4096]{1,0:T(8,128)(2,1)S(1)}, u32[]{:S(2)}, u32[]{:S(2)}) collective-permute-start(bf16[16,4096]{1,0:T(8,128)(2,1)S(1)} %get-tuple-element.10), channel_id=1, source_target_pairs={{0,4},{4,8},{8,12},{12,0},{1,5},{5,9},{9,13},{13,1},{2,6},{6,10},{... | collective-permute-start | bytes 393224 | tf_op jit(solution)/shard_map/ppermute | solution.py:103
  105.7 7.2 %collective-permute-start.6 = (bf16[16,4096]{1,0:T(8,128)(2,1)S(1)}, bf16[16,4096]{1,0:T(8,128)(2,1)S(1)}, u32[]{:S(2)}, u32[]{:S(2)}) collective-permute-start(bf16[16,4096]{1,0:T(8,128)(2,1)S(1)} %get-tuple-element.11), channel_id=1, source_target_pairs={{0,12},{4,0},{8,4},{12,8},{1,13},{5,1},{9,5},{13,9},{2,14},{6,2},{... | collective-permute-start | bytes 393224 | tf_op jit(solution)/shard_map/ppermute | solution.py:103
  108.2 8.4 %collective-permute-start.5 = (bf16[16,4096]{1,0:T(8,128)(2,1)S(1)}, bf16[16,4096]{1,0:T(8,128)(2,1)S(1)}, u32[]{:S(2)}, u32[]{:S(2)}) collective-permute-start(bf16[16,4096]{1,0:T(8,128)(2,1)S(1)} %get-tuple-element.12), channel_id=1, source_target_pairs={{0,8},{4,12},{8,0},{12,4},{1,9},{5,13},{9,1},{13,5},{2,10},{6,14},... | collective-permute-start | bytes 393224 | tf_op jit(solution)/shard_map/ppermute | solution.py:103

commit v3 on v2

--- a/solution.py
+++ b/solution.py
@@ -48,16 +48,18 @@
     n_y, n_z, n_x = lax.axis_size("ylo"), lax.axis_size("z"), lax.axis_size("x")
     block = width // (n_y * n_z)
 
+    me_h = lax.axis_index("yhi")
     cols = upstream_grad.reshape(rows, n_y, n_z * block).transpose(1, 0, 2)
-    me_h = lax.axis_index("yhi")
-    cols = jnp.broadcast_to(cols[:, None], (n_y, 2, rows, n_z * block))
-    cols = lax.all_to_all(cols.reshape(2 * n_y, rows, -1), ("ylo", "yhi"), 0, 0)
-    cols = cols.reshape(n_y, 2, rows, n_z * block).transpose(1, 2, 0, 3).reshape(2 * rows, width)
+    cols = jnp.broadcast_to(cols[:, None], (n_y, 4, rows, n_z * block))
+    cols = lax.all_to_all(cols.reshape(4 * n_y, rows, -1), ("ylo", "yhi", "core"), 0, 0)
+    cols = cols.reshape(n_y, 2, 2, rows, n_z * block).transpose(2, 1, 3, 0, 4)
+    cols = cols.reshape(2, 2 * rows, width)
+    cols = in_order(cols[0], cols[1], lax.axis_index("core"))
 
     other = swap(jnp.concatenate([tokens, upstream_grad], axis=0), "yhi")
     tokens2 = in_order(tokens, other[:rows], me_h)
     upstream2 = in_order(upstream_grad, other[rows:], me_h)
-    pair = jnp.stack([upstream2, cols], axis=0)[None]
+    pair = jnp.concatenate([upstream2, cols], axis=0).reshape(1, 3, 2 * rows, width)
 
     tokens_x = lax.all_gather(tokens2, "x", axis=0, tiled=True)
     gathered = both(tokens_x, "core")
@@ -70,7 +72,7 @@
 
     hidden_y = lax.all_gather(hidden, "ylo", axis=0)
     pair_x = after(pair_x, hidden_y)
-    cols = both(pair_x[:, 1].reshape(-1, width), "core").reshape(-1, n_y, n_z * block)
+    cols = pair_x[:, 1:].transpose(1, 0, 2, 3).reshape(-1, n_y, n_z * block)
     factor = float(n_z * cols.shape[0] * n_y) ** (-0.5)
     down = lax.dot_general(
         hidden_y, cols, (((0, 1), (1, 0)), ((), ())), preferred_element_type=jnp.float32
@@ -78,7 +80,7 @@
     down = (down * factor).astype(jnp.bfloat16).reshape(f_dev, n_z, block).transpose(1, 0, 2)
     down_z = lax.all_to_all(down, "z", 0, 0)
 
-    upstream = both(after(pair_x, down)[:, 0].reshape(-1, width), "core")
+    upstream = both(after(pair_x[:, 0].reshape(-1, width), down), "core")
     grad_hidden = contract_cols(upstream, w_down).astype(jnp.bfloat16)
     hidden_f = grad_hidden.astype(jnp.float32)
     grad_gate = (hidden_f * up_pre * sig_gate * (1.0 + gate_pre * (1.0 - sig_gate))).astype(

time: 136 us -> 134 us (0.985)
  the two profiles are of different devices: /device:TPU:2 before, /device:TPU:1 now
where the time goes in v3:
time: 134 us; the launch traced here: 133 us
  starting transfers between devices  47.4 us (35%)
  blocking collectives  41.7 us (31%)
  matrix products  18.8 us (14%)
  waiting for transfers between devices  11.1 us (8%)
  local copies, waits for them, and re-layouts  8.12 us (6%)
  other arithmetic  5.23 us (4%)
    all_gather x1, blocking collectives, body(): hidden_y = lax.all_gather(hidden, 'ylo', axis=0)  18.6 us
    ppermute x3, starting transfers between devices, swap(): return lax.ppermute(value, axis, SWAP)  17.8 us
    dot_general x3, matrix products, contract_cols(): lax.dot_general(left, right, (((1,), (1,)), ((), ())), preferred_element_...  10.9 us
    all_gather x1, blocking collectives, body(): tokens_x = lax.all_gather(tokens2, 'x', axis=0, tiled=True)  10.6 us
    ppermute x3, starting transfers between devices, body(): piece = lax.ppermute(piece, 'x', [(i, (i + k) % n_x) for i in range(n_x)])  10.5 us
    all_gather x1, blocking collectives, body(): sent = lax.all_gather(sent, 'yhi', axis=0)  8.1 us
    all_to_all x1, starting transfers between devices, body(): down_z = lax.all_to_all(down, 'z', 0, 0)  7.79 us
    all_to_all x1, starting transfers between devices, body(): lax.all_to_all(cols.reshape(4 * n_y, rows, -1), ('ylo', 'yhi', 'core'), 0...  7.73 us
  transfers between devices with their start and end apart: 9, of which 2 were waited for; matrix products, arithmetic and copies ran while one was open for 18% of the time, Pallas kernels for 0%

profile of v3, /device:TPU:1, one launch (start us, length us, event | category | flops | bytes accessed | tf_op | source)
XLA Modules:
  0.0 133.4 jit_solution(1417134557034893310)
XLA Ops:
  0.6 0.9 pad_maximum_fusion.1
  1.5 8.3 %collective-permute-start = (bf16[16,4096]{1,0:T(8,128)(2,1)S(1)}, bf16[16,4096]{1,0:T(8,128)(2,1)S(1)}, u32[]{:S(2)}, u32[]{:S(2)}) collective-permute-start(bf16[16,4096]{1,0:T(8,128)(2,1)S(1)} %pad_maximum_fusion.1), channel_id=1, source_target_pairs={{0,2},{2,0},{1,3},{3,1},{4,6},{6,4},{5,7},{7,5},{8,10},{10,8},{9,1... | collective-permute-start | bytes 393224 | tf_op jit(solution)/shard_map/ppermute | solution.py:24
  9.8 1.6 %broadcast_in_dim.6 = bf16[4,4,8,1024]{3,2,1,0:T(8,128)(2,1)} broadcast(bf16[4,8,1024]{2,1,0:T(8,128)(2,1)} %bitcast.67), dimensions={0,2,3} | broadcast | bytes 327680 | tf_op jit(solution)/shard_map/broadcast_in_dim | solution.py:53
  11.4 7.7 %all-to-all-start = ((bf16[16,8,1024]{2,1,0:T(8,128)(2,1)}), bf16[16,8,1024]{2,1,0:T(8,128)(2,1)S(1)}, u32[]{:S(2)}, u32[]{:S(2)}) async-start(bf16[16,8,1024]{2,1,0:T(8,128)(2,1)} %bitcast.2), calls=%async_computation | async-start | bytes 524288 | tf_op jit(solution)/shard_map/all_to_all | solution.py:54
  19.1 0.9 broadcast_select_fusion.5
  20.0 10.6 %all_gather.25 = bf16[64,4096]{1,0:T(8,128)(2,1)S(1)} all-gather(bf16[16,4096]{1,0:T(8,128)(2,1)S(1)} %pad_maximum_fusion.2), channel_id=1, replica_groups=mesh['ylo'=4,'z'=8,'x'=4,'yhi'=2,'core'=2] {'x'}, dimensions={0}, use_global_device_ids=true | all-gather | bytes 655360 | tf_op jit(solution)/shard_map/all_gather | solution.py:64
  30.6 5.8 %collective-permute-start.1 = (bf16[64,4096]{1,0:T(8,128)(2,1)S(1)}, bf16[64,4096]{1,0:T(8,128)(2,1)}, u32[]{:S(2)}, u32[]{:S(2)}) collective-permute-start(bf16[64,4096]{1,0:T(8,128)(2,1)S(1)} %all_gather.25), channel_id=1, source_target_pairs={{0,1},{1,0},{2,3},{3,2},{4,5},{5,4},{6,7},{7,6},{8,9},{9,8},{10,11... | collective-permute-start | bytes 1572872 | tf_op jit(solution)/shard_map/ppermute | solution.py:24
  36.8 1.4 %broadcast_in_dim.15 = bf16[4,3,16,4096]{3,2,1,0:T(8,128)(2,1)} broadcast(bf16[3,16,4096]{2,1,0:T(8,128)(2,1)S(1)} %bitcast.62), dimensions={1,2,3} | broadcast | bytes 1966080 | tf_op jit(solution)/shard_map/broadcast_in_dim | solution.py:32
  38.2 3.6 %all-to-all-start.1 = ((bf16[4,3,16,4096]{3,2,1,0:T(8,128)(2,1)}), bf16[4,3,16,4096]{3,2,1,0:T(8,128)(2,1)S(1)}, u32[]{:S(2)}, u32[]{:S(2)}) async-start(bf16[4,3,16,4096]{3,2,1,0:T(8,128)(2,1)} %broadcast_in_dim.15), calls=%async_computation.1 | async-start | bytes 3145728 | tf_op jit(solution)/shard_map/all_to_all | solution.py:33
  41.8 1.2 constant_dynamic-update-slice_fusion
  43.1 4.5 %fusion.17 = f32[128,896]{1,0:T(8,128)S(1)} fusion(bf16[128,4096]{1,0:T(8,128)(2,1)S(1)} %constant_dynamic-update-slice_fusion, bf16[4096,896]{1,0:T(8,128)(2,1)} %param.7), kind=kOutput, calls=%fused_computation.48 | convolution fusion | flops 939524096 | bytes 8847360 | tf_op jit(solution)/shard_map/dot_general | solution.py:67
  47.6 2.1 %multiply_convert_fusion.2 = (bf16[128,896]{1,0:T(8,128)(2,1)S(1)}, f32[128,896]{1,0:T(8,128)}) fusion(f32[128,896]{1,0:T(8,128)S(1)} %fusion.17, bf16[128,4096]{1,0:T(8,128)(2,1)S(1)} %constant_dynamic-update-slice_fusion, bf16[4096,896]{1,0:T(8,128)(2,1)S(1)} %bitcast.58), kind=kOutput, calls=%fused_computation.17 | convolution fusion | flops 940212224 | bytes 9535488 | tf_op jit(solution)/shard_map/dot_general | solution.py:68
  49.7 18.6 %all-gather = bf16[512,896]{1,0:T(8,128)(2,1)S(1)} all-gather(bf16[128,896]{1,0:T(8,128)(2,1)S(1)} %get-tuple-element.21), channel_id=2, replica_groups=mesh['ylo'=4,'z'=8,'x'=4,'yhi'=2,'core'=2] {'ylo'}, dimensions={0}, use_global_device_ids=true | all-gather | bytes 1146880 | tf_op jit(solution)/shard_map/all_gather | solution.py:73
  68.4 0.8 slice.33
  69.4 0.8 reshape.42
  70.2 1.3 fusion.2
  71.5 1.6 %copy.29 = bf16[112,8,8,128]{3,2,0,1:T(8,128)(2,1)} copy(bf16[112,8,8,128]{3,2,1,0:T(8,128)(2,1)S(1)} %fusion.2) | data formatting | bytes 3670016 | tf_op jit(solution)/shard_map/reshape | solution.py:80
  73.1 3.8 %collective-permute-start.2 = (bf16[64,4096]{1,0:T(8,128)(2,1)}, bf16[64,4096]{1,0:T(8,128)(2,1)}, u32[]{:S(2)}, u32[]{:S(2)}) collective-permute-start(bf16[64,4096]{1,0:T(8,128)(2,1)} %bitcast.9), channel_id=1, source_target_pairs={{0,1},{1,0},{2,3},{3,2},{4,5},{5,4},{6,7},{7,6},{8,9},{9,8},{10,11... | collective-permute-start | bytes 1572872 | tf_op jit(solution)/shard_map/ppermute | solution.py:24
  76.9 7.8 %all-to-all-start.2 = ((bf16[8,896,128]{2,1,0:T(8,128)(2,1)}), bf16[8,896,128]{2,1,0:T(8,128)(2,1)}, u32[]{:S(2)}, u32[]{:S(2)}) async-start(bf16[8,896,128]{2,1,0:T(8,128)(2,1)} %bitcast.61), calls=%async_computation.2 | async-start | bytes 3670016 | tf_op jit(solution)/shard_map/all_to_all | solution.py:81
  84.7 6.0 %fusion.3 = f32[128,896]{1,0:T(8,128)S(1)} fusion(bf16[896,4096]{1,0:T(8,128)(2,1)} %param.9, bf16[64,4096]{1,0:T(8,128)(2,1)} %collective-permute-done.2, bf16[64,4096]{1,0:T(8,128)(2,1)} %bitcast.9), kind=kOutput, calls=%fused_computation.8 | convolution fusion | flops 941850624 | bytes 8847360 | tf_op jit(solution)/shard_map/dot_general | solution.py:18
  90.8 2.4 %fusion.9 = f32[128,4096]{1,0:T(8,128)S(1)} fusion(bf16[4096,896]{1,0:T(8,128)(2,1)S(1)} %bitcast.56, f32[128,896]{1,0:T(8,128)S(1)} %copy-done.1, f32[128,896]{1,0:T(8,128)S(1)} %fusion.3, f32[128,896]{1,0:T(8,128)S(1)} %copy-done.2), kind=kOutput, calls=%fused_computation.24 | convolution fusion | flops 940670976 | bytes 10813440 | tf_op jit(solution)/shard_map/dot_general | solution.py:18
  93.2 2.5 %fusion = bf16[128,4096]{1,0:T(8,128)(2,1)S(1)} fusion(f32[128,4096]{1,0:T(8,128)S(1)} %fusion.9, bf16[4096,896]{1,0:T(8,128)(2,1)S(1)} %bitcast.60, f32[128,896]{1,0:T(8,128)S(1)} %fusion.3, f32[128,896]{1,0:T(8,128)S(1)} %copy-done.1), kind=kOutput, calls=%fused_computation.1 | convolution fusion | flops 941260800 | bytes 11403264 | tf_op jit(solution)/shard_map/dot_general | solution.py:18
  95.8 2.2 %all-gather.1 = bf16[128,2048]{1,0:T(8,128)(2,1)S(1)} all-gather(bf16[64,2048]{1,0:T(8,128)(2,1)S(1)} %get-tuple-element.8), channel_id=3, replica_groups=mesh['ylo'=4,'z'=8,'x'=4,'yhi'=2,'core'=2] {'core'}, dimensions={0}, use_global_device_ids=true | all-gather | bytes 786432 | tf_op jit(solution)/shard_map/all_gather | solution.py:96
  97.9 2.2 %all-gather.2 = bf16[128,2048]{1,0:T(8,128)(2,1)S(1)} all-gather(bf16[64,2048]{1,0:T(8,128)(2,1)S(1)} %get-tuple-element.9), channel_id=4, replica_groups=mesh['ylo'=4,'z'=8,'x'=4,'yhi'=2,'core'=2] {'core'}, dimensions={0}, use_global_device_ids=true | all-gather | bytes 786432 | tf_op jit(solution)/shard_map/all_gather | solution.py:96
  100.3 3.7 %collective-permute-start.3 = (bf16[16,4096]{1,0:T(8,128)(2,1)S(1)}, bf16[16,4096]{1,0:T(8,128)(2,1)S(1)}, u32[]{:S(2)}, u32[]{:S(2)}) collective-permute-start(bf16[16,4096]{1,0:T(8,128)(2,1)S(1)} %get-tuple-element.10), channel_id=1, source_target_pairs={{0,4},{4,8},{8,12},{12,0},{1,5},{5,9},{9,13},{13,1},{2,6},{6,10},{... | collective-permute-start | bytes 393224 | tf_op jit(solution)/shard_map/ppermute | solution.py:105
  104.1 3.1 %collective-permute-start.5 = (bf16[16,4096]{1,0:T(8,128)(2,1)S(1)}, bf16[16,4096]{1,0:T(8,128)(2,1)S(1)}, u32[]{:S(2)}, u32[]{:S(2)}) collective-permute-start(bf16[16,4096]{1,0:T(8,128)(2,1)S(1)} %get-tuple-element.11), channel_id=1, source_target_pairs={{0,12},{4,0},{8,4},{12,8},{1,13},{5,1},{9,5},{13,9},{2,14},{6,2},{... | collective-permute-start | bytes 393224 | tf_op jit(solution)/shard_map/ppermute | solution.py:105
  107.2 3.7 %collective-permute-start.4 = (bf16[16,4096]{1,0:T(8,128)(2,1)S(1)}, bf16[16,4096]{1,0:T(8,128)(2,1)S(1)}, u32[]{:S(2)}, u32[]{:S(2)}) collective-permute-start(bf16[16,4096]{1,0:T(8,128)(2,1)S(1)} %get-tuple-element.12), channel_id=1, source_target_pairs={{0,8},{4,12},{8,0},{12,4},{1,9},{5,13},{9,1},{13,5},{2,10},{6,14},... | collective-permute-start | bytes 393224 | tf_op jit(solution)/shard_map/ppermute | solution.py:105
  110.9 4.2 %collective-permute-done.4 = bf16[16,4096]{1,0:T(8,128)(2,1)S(1)} collective-permute-done((bf16[16,4096]{1,0:T(8,128)(2,1)S(1)}, bf16[16,4096]{1,0:T(8,128)(2,1)S(1)}, u32[]{:S(2)}, u32[]{:S(2)}) %collective-permute-start.4) | collective-permute-done | bytes 131104 | tf_op jit(solution)/shard_map/ppermute | solution.py:105
  115.2 8.1 %all_gather.32 = bf16[2,8,4096]{2,1,0:T(8,128)(2,1)S(1)} all-gather(bf16[1,8,4096]{2,1,0:T(8,128)(2,1)S(1)} %dynamic-slice_convert_fusion), channel_id=1, replica_groups=mesh['ylo'=4,'z'=8,'x'=4,'yhi'=2,'core'=2] {'yhi'}, dimensions={0}, use_global_device_ids=true | all-gather | bytes 196608 | tf_op jit(solution)/shard_map/all_gather | solution.py:110
  123.3 0.6 fusion.12
  123.9 6.9 %all-to-all-done.2 = bf16[8,896,128]{2,1,0:T(8,128)(2,1)} async-done(((bf16[8,896,128]{2,1,0:T(8,128)(2,1)}), bf16[8,896,128]{2,1,0:T(8,128)(2,1)}, u32[]{:S(2)}, u32[]{:S(2)}) %all-to-all-start.2) | async-done | bytes 1835040 | tf_op jit(solution)/shard_map/all_to_all | solution.py:81
  130.8 2.6 %convert_reduce_fusion = f32[896,128]{1,0:T(8,128)} fusion(bf16[8,896,128]{2,1,0:T(8,128)(2,1)} %all-to-all-done.2), kind=kLoop, calls=%fused_computation.4 | loop fusion | flops 1720320 | bytes 2293760 | tf_op jit(solution)/shard_map/reduce_sum | solution.py:114
  (44 shorter events, 1.0 us)
Async XLA Ops:
  1.5 17.6 %collective-permute-start = (bf16[16,4096]{1,0:T(8,128)(2,1)S(1)}, bf16[16,4096]{1,0:T(8,128)(2,1)S(1)}, u32[]{:S(2)}, u32[]{:S(2)}) collective-permute-start(bf16[16,4096]{1,0:T(8,128)(2,1)S(1)} %pad_maximum_fusion.1), channel_id=1, source_target_pairs={{0,2},{2,0},{1,3},{3,1},{4,6},{6,4},{5,7},{7,5},{8,10},{10,8},{9,1... | collective-permute-start | bytes 393224 | tf_op jit(solution)/shard_map/ppermute | solution.py:24
  11.4 25.1 %all-to-all-start = ((bf16[16,8,1024]{2,1,0:T(8,128)(2,1)}), bf16[16,8,1024]{2,1,0:T(8,128)(2,1)S(1)}, u32[]{:S(2)}, u32[]{:S(2)}) async-start(bf16[16,8,1024]{2,1,0:T(8,128)(2,1)} %bitcast.2), calls=%async_computation | async-start | bytes 524288 | tf_op jit(solution)/shard_map/all_to_all | solution.py:54
  30.6 11.2 %collective-permute-start.1 = (bf16[64,4096]{1,0:T(8,128)(2,1)S(1)}, bf16[64,4096]{1,0:T(8,128)(2,1)}, u32[]{:S(2)}, u32[]{:S(2)}) collective-permute-start(bf16[64,4096]{1,0:T(8,128)(2,1)S(1)} %all_gather.25), channel_id=1, source_target_pairs={{0,1},{1,0},{2,3},{3,2},{4,5},{5,4},{6,7},{7,6},{8,9},{9,8},{10,11... | collective-permute-start | bytes 1572872 | tf_op jit(solution)/shard_map/ppermute | solution.py:24
  38.2 30.1 %all-to-all-start.1 = ((bf16[4,3,16,4096]{3,2,1,0:T(8,128)(2,1)}), bf16[4,3,16,4096]{3,2,1,0:T(8,128)(2,1)S(1)}, u32[]{:S(2)}, u32[]{:S(2)}) async-start(bf16[4,3,16,4096]{3,2,1,0:T(8,128)(2,1)} %broadcast_in_dim.15), calls=%async_computation.1 | async-start | bytes 3145728 | tf_op jit(solution)/shard_map/all_to_all | solution.py:33
  41.8 5.8 %slice-start.2 = ((s8[7340032]{0:T(1024)(128)(4,1)}), s8[4194304]{0:T(1024)(128)(4,1)S(1)}, s32[]{:S(2)}) async-start(s8[7340032]{0:T(1024)(128)(4,1)} %bitcast.57), calls=%async_computation.5 | async-start | bytes 8388608
  43.0 4.6 %slice-start.3 = ((s8[7340032]{0:T(1024)(128)(4,1)}), s8[3145728]{0:T(1024)(128)(4,1)S(1)}, s32[]{:S(2)}) async-start(s8[7340032]{0:T(1024)(128)(4,1)} %bitcast.57), calls=%async_computation.6 | async-start | bytes 6291456
  47.6 2.1 %copy-start = (f32[128,896]{1,0:T(8,128)}, f32[128,896]{1,0:T(8,128)S(1)}, u32[]{:S(2)}) copy-start(f32[128,896]{1,0:T(8,128)S(1)} %fusion.17) | copy-start | bytes 1376260
  71.5 19.2 %slice-start = ((s8[7340032]{0:T(1024)(128)(4,1)}), s8[3145728]{0:T(1024)(128)(4,1)S(1)}, s32[]{:S(2)}) async-start(s8[7340032]{0:T(1024)(128)(4,1)} %bitcast.55), calls=%async_computation.3 | async-start | bytes 6291456
  73.1 11.6 %collective-permute-start.2 = (bf16[64,4096]{1,0:T(8,128)(2,1)}, bf16[64,4096]{1,0:T(8,128)(2,1)}, u32[]{:S(2)}, u32[]{:S(2)}) collective-permute-start(bf16[64,4096]{1,0:T(8,128)(2,1)} %bitcast.9), channel_id=1, source_target_pairs={{0,1},{1,0},{2,3},{3,2},{4,5},{5,4},{6,7},{7,6},{8,9},{9,8},{10,11... | collective-permute-start | bytes 1572872 | tf_op jit(solution)/shard_map/ppermute | solution.py:24
  76.9 54.0 %all-to-all-start.2 = ((bf16[8,896,128]{2,1,0:T(8,128)(2,1)}), bf16[8,896,128]{2,1,0:T(8,128)(2,1)}, u32[]{:S(2)}, u32[]{:S(2)}) async-start(bf16[8,896,128]{2,1,0:T(8,128)(2,1)} %bitcast.61), calls=%async_computation.2 | async-start | bytes 3670016 | tf_op jit(solution)/shard_map/all_to_all | solution.py:81
  84.6 6.1 %slice-start.1 = ((s8[7340032]{0:T(1024)(128)(4,1)}), s8[4194304]{0:T(1024)(128)(4,1)S(1)}, s32[]{:S(2)}) async-start(s8[7340032]{0:T(1024)(128)(4,1)} %bitcast.55), calls=%async_computation.4 | async-start | bytes 8388608
  84.7 6.1 %copy-start.1 = (f32[128,896]{1,0:T(8,128)S(1)}, f32[128,896]{1,0:T(8,128)}, u32[]{:S(2)}) copy-start(f32[128,896]{1,0:T(8,128)} %copy-done) | copy-start | bytes 1376260
  84.7 6.1 %copy-start.2 = (f32[128,896]{1,0:T(8,128)S(1)}, f32[128,896]{1,0:T(8,128)}, u32[]{:S(2)}) copy-start(f32[128,896]{1,0:T(8,128)} %get-tuple-element.22) | copy-start | bytes 1376260
  84.7 8.5 %slice-start.4 = ((s8[7340032]{0:T(1024)(128)(4,1)}), s8[4194304]{0:T(1024)(128)(4,1)S(1)}, s32[]{:S(2)}) async-start(s8[7340032]{0:T(1024)(128)(4,1)} %bitcast.59), calls=%async_computation.7 | async-start | bytes 8388608
  90.7 2.5 %slice-start.5 = ((s8[7340032]{0:T(1024)(128)(4,1)}), s8[3145728]{0:T(1024)(128)(4,1)S(1)}, s32[]{:S(2)}) async-start(s8[7340032]{0:T(1024)(128)(4,1)} %bitcast.59), calls=%async_computation.8 | async-start | bytes 6291456
  100.3 10.5 %collective-permute-start.3 = (bf16[16,4096]{1,0:T(8,128)(2,1)S(1)}, bf16[16,4096]{1,0:T(8,128)(2,1)S(1)}, u32[]{:S(2)}, u32[]{:S(2)}) collective-permute-start(bf16[16,4096]{1,0:T(8,128)(2,1)S(1)} %get-tuple-element.10), channel_id=1, source_target_pairs={{0,4},{4,8},{8,12},{12,0},{1,5},{5,9},{9,13},{13,1},{2,6},{6,10},{... | collective-permute-start | bytes 393224 | tf_op jit(solution)/shard_map/ppermute | solution.py:105
  104.1 6.8 %collective-permute-start.5 = (bf16[16,4096]{1,0:T(8,128)(2,1)S(1)}, bf16[16,4096]{1,0:T(8,128)(2,1)S(1)}, u32[]{:S(2)}, u32[]{:S(2)}) collective-permute-start(bf16[16,4096]{1,0:T(8,128)(2,1)S(1)} %get-tuple-element.11), channel_id=1, source_target_pairs={{0,12},{4,0},{8,4},{12,8},{1,13},{5,1},{9,5},{13,9},{2,14},{6,2},{... | collective-permute-start | bytes 393224 | tf_op jit(solution)/shard_map/ppermute | solution.py:105
  107.2 7.9 %collective-permute-start.4 = (bf16[16,4096]{1,0:T(8,128)(2,1)S(1)}, bf16[16,4096]{1,0:T(8,128)(2,1)S(1)}, u32[]{:S(2)}, u32[]{:S(2)}) collective-permute-start(bf16[16,4096]{1,0:T(8,128)(2,1)S(1)} %get-tuple-element.12), channel_id=1, source_target_pairs={{0,8},{4,12},{8,0},{12,4},{1,9},{5,13},{9,1},{13,5},{2,10},{6,14},... | collective-permute-start | bytes 393224 | tf_op jit(solution)/shard_map/ppermute | solution.py:105

commit v4 on v3

--- a/solution.py
+++ b/solution.py
@@ -62,7 +62,8 @@
     pair = jnp.concatenate([upstream2, cols], axis=0).reshape(1, 3, 2 * rows, width)
 
     tokens_x = lax.all_gather(tokens2, "x", axis=0, tiled=True)
-    gathered = both(tokens_x, "core")
+    gathered = tokens_x.reshape(n_x, 1, 2 * rows, width)
+    gathered = jnp.concatenate([gathered, swap(gathered, "core")], axis=1).reshape(-1, width)
     pair_x = gather_a2a(after(pair, tokens_x), "x")
     gate_pre = jnp.dot(gathered, w_gate, preferred_element_type=jnp.float32)
     up_pre = jnp.dot(gathered, w_up, preferred_element_type=jnp.float32)
@@ -72,7 +73,7 @@
 
     hidden_y = lax.all_gather(hidden, "ylo", axis=0)
     pair_x = after(pair_x, hidden_y)
-    cols = pair_x[:, 1:].transpose(1, 0, 2, 3).reshape(-1, n_y, n_z * block)
+    cols = pair_x[:, 1:].reshape(-1, n_y, n_z * block)
     factor = float(n_z * cols.shape[0] * n_y) ** (-0.5)
     down = lax.dot_general(
         hidden_y, cols, (((0, 1), (1, 0)), ((), ())), preferred_element_type=jnp.float32
@@ -80,7 +81,8 @@
     down = (down * factor).astype(jnp.bfloat16).reshape(f_dev, n_z, block).transpose(1, 0, 2)
     down_z = lax.all_to_all(down, "z", 0, 0)
 
-    upstream = both(after(pair_x[:, 0].reshape(-1, width), down), "core")
+    upstream = after(pair_x[:, :1], down)
+    upstream = jnp.concatenate([upstream, swap(upstream, "core")], axis=1).reshape(-1, width)
     grad_hidden = contract_cols(upstream, w_down).astype(jnp.bfloat16)
     hidden_f = grad_hidden.astype(jnp.float32)
     grad_gate = (hidden_f * up_pre * sig_gate * (1.0 + gate_pre * (1.0 - sig_gate))).astype(
@@ -89,14 +91,15 @@
     grad_up = (hidden_f * act_gate).astype(jnp.bfloat16)
     partial = (contract_cols(grad_gate, w_gate) + contract_cols(grad_up, w_up)).astype(jnp.bfloat16)
 
-    half = partial.shape[0] // 2
+    partial = partial.reshape(n_x, 2, 2 * rows, width)
+    away, partial = (partial[:, k].reshape(-1, width) for k in (1, 0))
     other = []
     for k in range(2):
-        cut = partial[half:, k * width // 2 : (k + 1) * width // 2]
+        cut = away[:, k * width // 2 : (k + 1) * width // 2]
         cut = lax.all_gather(cut, "core", axis=0)
         other.append(lax.dynamic_index_in_dim(cut, 1 - lax.axis_index("core"), 0, keepdims=False))
     other = jnp.concatenate(other, axis=1)
-    partial = (partial[:half].astype(jnp.float32) + other.astype(jnp.float32)).astype(jnp.bfloat16)
+    partial = (partial.astype(jnp.float32) + other.astype(jnp.float32)).astype(jnp.bfloat16)
     me = lax.axis_index("x")
     chunk = 2 * rows
     total = lax.dynamic_slice_in_dim(partial, me * chunk, chunk, 0).astype(jnp.float32)

time: 134 us -> 133 us (level)
  other arithmetic: 5.23 us -> 6.76 us
    concatenate x0 -> x2, other arithmetic: none -> 1.48 us  [the longest x1 1.38 us: body(): jnp.concatenate([upstream, swap(upstream, 'core')], axis=1)]
where the time goes in v4:
time: 133 us
  starting transfers between devices  47.5 us (36%)
  blocking collectives  41.7 us (31%)
  matrix products  18.5 us (14%)
  waiting for transfers between devices  9.89 us (7%)
  local copies, waits for them, and re-layouts  7.43 us (6%)
  other arithmetic  6.76 us (5%)
    all_gather x1, blocking collectives, body(): hidden_y = lax.all_gather(hidden, 'ylo', axis=0)  18.6 us
    ppermute x3, starting transfers between devices, swap(): return lax.ppermute(value, axis, SWAP)  17.7 us
    dot_general x3, matrix products, contract_cols(): lax.dot_general(left, right, (((1,), (1,)), ((), ())), preferred_element_...  10.6 us
    all_gather x1, blocking collectives, body(): tokens_x = lax.all_gather(tokens2, 'x', axis=0, tiled=True)  10.6 us
    ppermute x3, starting transfers between devices, body(): piece = lax.ppermute(piece, 'x', [(i, (i + k) % n_x) for i in range(n_x)])  10.5 us
    all_gather x1, blocking collectives, body(): sent = lax.all_gather(sent, 'yhi', axis=0)  8.1 us
    all_to_all x1, starting transfers between devices, body(): down_z = lax.all_to_all(down, 'z', 0, 0)  8.04 us
    all_to_all x1, starting transfers between devices, body(): lax.all_to_all(cols.reshape(4 * n_y, rows, -1), ('ylo', 'yhi', 'core'), 0...  7.73 us
  transfers between devices with their start and end apart: 9, of which 2 were waited for; matrix products, arithmetic and copies ran while one was open for 18% of the time, Pallas kernels for 0%

profile of v4, /device:TPU:1, one launch (start us, length us, event | category | flops | bytes accessed | tf_op | source)
XLA Modules:
  0.0 132.8 jit_solution(7418696291204470429)
XLA Ops:
  0.6 0.9 pad_maximum_fusion.3
  1.5 8.3 %collective-permute-start = (bf16[16,4096]{1,0:T(8,128)(2,1)S(1)}, bf16[16,4096]{1,0:T(8,128)(2,1)S(1)}, u32[]{:S(2)}, u32[]{:S(2)}) collective-permute-start(bf16[16,4096]{1,0:T(8,128)(2,1)S(1)} %pad_maximum_fusion.3), channel_id=1, source_target_pairs={{0,2},{2,0},{1,3},{3,1},{4,6},{6,4},{5,7},{7,5},{8,10},{10,8},{9,1... | collective-permute-start | bytes 393224 | tf_op jit(solution)/shard_map/ppermute | solution.py:24
  9.8 1.6 %broadcast_in_dim.6 = bf16[4,4,8,1024]{3,2,1,0:T(8,128)(2,1)} broadcast(bf16[4,8,1024]{2,1,0:T(8,128)(2,1)} %bitcast.83), dimensions={0,2,3} | broadcast | bytes 327680 | tf_op jit(solution)/shard_map/broadcast_in_dim | solution.py:53
  11.4 7.7 %all-to-all-start = ((bf16[16,8,1024]{2,1,0:T(8,128)(2,1)}), bf16[16,8,1024]{2,1,0:T(8,128)(2,1)S(1)}, u32[]{:S(2)}, u32[]{:S(2)}) async-start(bf16[16,8,1024]{2,1,0:T(8,128)(2,1)} %bitcast.2), calls=%async_computation | async-start | bytes 524288 | tf_op jit(solution)/shard_map/all_to_all | solution.py:54
  19.1 0.9 broadcast_select_fusion.5
  20.0 10.6 %all_gather.25 = bf16[64,4096]{1,0:T(8,128)(2,1)S(1)} all-gather(bf16[16,4096]{1,0:T(8,128)(2,1)S(1)} %pad_maximum_fusion.4), channel_id=1, replica_groups=mesh['ylo'=4,'z'=8,'x'=4,'yhi'=2,'core'=2] {'x'}, dimensions={0}, use_global_device_ids=true | all-gather | bytes 655360 | tf_op jit(solution)/shard_map/all_gather | solution.py:64
  30.6 5.8 %collective-permute-start.1 = (bf16[4,1,16,4096]{3,2,1,0:T(8,128)(2,1)S(1)}, bf16[4,1,16,4096]{3,2,1,0:T(8,128)(2,1)S(1)}, u32[]{:S(2)}, u32[]{:S(2)}) collective-permute-start(bf16[4,1,16,4096]{3,2,1,0:T(8,128)(2,1)S(1)} %bitcast.75), channel_id=1, source_target_pairs={{0,1},{1,0},{2,3},{3,2},{4,5},{5,4},{6,7},{7,6},{8,9},{9,8},{10,11... | collective-permute-start | bytes 1572872 | tf_op jit(solution)/shard_map/ppermute | solution.py:24
  36.8 1.4 %broadcast_in_dim.15 = bf16[4,3,16,4096]{3,2,1,0:T(8,128)(2,1)} broadcast(bf16[3,16,4096]{2,1,0:T(8,128)(2,1)S(1)} %bitcast.78), dimensions={1,2,3} | broadcast | bytes 1966080 | tf_op jit(solution)/shard_map/broadcast_in_dim | solution.py:32
  38.2 3.6 %all-to-all-start.1 = ((bf16[4,3,16,4096]{3,2,1,0:T(8,128)(2,1)}), bf16[4,3,16,4096]{3,2,1,0:T(8,128)(2,1)S(1)}, u32[]{:S(2)}, u32[]{:S(2)}) async-start(bf16[4,3,16,4096]{3,2,1,0:T(8,128)(2,1)} %broadcast_in_dim.15), calls=%async_computation.1 | async-start | bytes 3145728 | tf_op jit(solution)/shard_map/all_to_all | solution.py:33
  41.9 4.5 %fusion.15 = f32[128,896]{1,0:T(8,128)S(1)} fusion(bf16[128,4096]{1,0:T(8,128)(2,1)S(1)} %bitcast.70, bf16[4096,896]{1,0:T(8,128)(2,1)} %param.7), kind=kOutput, calls=%fused_computation.45 | convolution fusion | flops 939524096 | bytes 8847360 | tf_op jit(solution)/shard_map/dot_general | solution.py:68
  47.0 2.1 %multiply_convert_fusion.2 = (bf16[128,896]{1,0:T(8,128)(2,1)S(1)}, f32[128,896]{1,0:T(8,128)}) fusion(f32[128,896]{1,0:T(8,128)S(1)} %fusion.15, bf16[128,4096]{1,0:T(8,128)(2,1)S(1)} %bitcast.71, bf16[4096,896]{1,0:T(8,128)(2,1)S(1)} %bitcast.67), kind=kOutput, calls=%fused_computation.16 | convolution fusion | flops 940212224 | bytes 9535488 | tf_op jit(solution)/shard_map/dot_general | solution.py:69
  49.1 18.6 %all-gather = bf16[512,896]{1,0:T(8,128)(2,1)S(1)} all-gather(bf16[128,896]{1,0:T(8,128)(2,1)S(1)} %get-tuple-element.23), channel_id=2, replica_groups=mesh['ylo'=4,'z'=8,'x'=4,'yhi'=2,'core'=2] {'ylo'}, dimensions={0}, use_global_device_ids=true | all-gather | bytes 1146880 | tf_op jit(solution)/shard_map/all_gather | solution.py:74
  67.8 0.8 slice.36
  68.7 0.8 reshape.58
  69.5 1.3 fusion.2
  70.8 1.6 %copy.32 = bf16[112,8,8,128]{3,2,0,1:T(8,128)(2,1)} copy(bf16[112,8,8,128]{3,2,1,0:T(8,128)(2,1)S(1)} %fusion.2) | data formatting | bytes 3670016 | tf_op jit(solution)/shard_map/reshape | solution.py:81
  72.3 3.6 %collective-permute-start.2 = (bf16[4,1,16,4096]{3,2,1,0:T(8,128)(2,1)}, bf16[4,1,16,4096]{3,2,1,0:T(8,128)(2,1)}, u32[]{:S(2)}, u32[]{:S(2)}) collective-permute-start(bf16[4,1,16,4096]{3,2,1,0:T(8,128)(2,1)} %slice.36), channel_id=1, source_target_pairs={{0,1},{1,0},{2,3},{3,2},{4,5},{5,4},{6,7},{7,6},{8,9},{9,8},{10,11... | collective-permute-start | bytes 1572872 | tf_op jit(solution)/shard_map/ppermute | solution.py:24
  76.0 8.0 %all-to-all-start.2 = ((bf16[8,896,128]{2,1,0:T(8,128)(2,1)}), bf16[8,896,128]{2,1,0:T(8,128)(2,1)}, u32[]{:S(2)}, u32[]{:S(2)}) async-start(bf16[8,896,128]{2,1,0:T(8,128)(2,1)} %bitcast.72), calls=%async_computation.2 | async-start | bytes 3670016 | tf_op jit(solution)/shard_map/all_to_all | solution.py:82
  84.1 1.4 %pad_maximum_fusion.1 = bf16[4,2,16,4096]{3,2,1,0:T(8,128)(2,1)S(1)} fusion(bf16[4,1,16,4096]{3,2,1,0:T(8,128)(2,1)} %collective-permute-done.2, bf16[4,1,16,4096]{3,2,1,0:T(8,128)(2,1)} %slice.36), kind=kLoop, calls=%fused_computation.10 | loop fusion | flops 524288 | bytes 2097152 | tf_op jit(solution)/shard_map/concatenate | solution.py:85
  85.5 5.7 %fusion.3 = f32[128,896]{1,0:T(8,128)S(1)} fusion(bf16[128,4096]{1,0:T(8,128)(2,1)S(1)} %bitcast.73, bf16[896,4096]{1,0:T(8,128)(2,1)} %param.9), kind=kOutput, calls=%fused_computation.8 | convolution fusion | flops 939753472 | bytes 8847360 | tf_op jit(solution)/shard_map/dot_general | solution.py:18
  91.2 2.4 %fusion.7 = f32[128,4096]{1,0:T(8,128)S(1)} fusion(bf16[4096,896]{1,0:T(8,128)(2,1)S(1)} %bitcast.65, f32[128,896]{1,0:T(8,128)S(1)} %copy-done.1, f32[128,896]{1,0:T(8,128)S(1)} %fusion.3, f32[128,896]{1,0:T(8,128)S(1)} %copy-done.2), kind=kOutput, calls=%fused_computation.23 | convolution fusion | flops 940670976 | bytes 10813440 | tf_op jit(solution)/shard_map/dot_general | solution.py:18
  93.7 2.5 %fusion = bf16[128,4096]{1,0:T(8,128)(2,1)S(1)} fusion(f32[128,4096]{1,0:T(8,128)S(1)} %fusion.7, bf16[4096,896]{1,0:T(8,128)(2,1)S(1)} %bitcast.69, f32[128,896]{1,0:T(8,128)S(1)} %fusion.3, f32[128,896]{1,0:T(8,128)S(1)} %copy-done.1), kind=kOutput, calls=%fused_computation.1 | convolution fusion | flops 941260800 | bytes 11403264 | tf_op jit(solution)/shard_map/dot_general | solution.py:18
  96.3 2.2 %all-gather.1 = bf16[128,2048]{1,0:T(8,128)(2,1)S(1)} all-gather(bf16[64,2048]{1,0:T(8,128)(2,1)S(1)} %get-tuple-element.13), channel_id=3, replica_groups=mesh['ylo'=4,'z'=8,'x'=4,'yhi'=2,'core'=2] {'core'}, dimensions={0}, use_global_device_ids=true | all-gather | bytes 786432 | tf_op jit(solution)/shard_map/all_gather | solution.py:99
  98.5 2.2 %all-gather.2 = bf16[128,2048]{1,0:T(8,128)(2,1)S(1)} all-gather(bf16[64,2048]{1,0:T(8,128)(2,1)S(1)} %get-tuple-element.14), channel_id=4, replica_groups=mesh['ylo'=4,'z'=8,'x'=4,'yhi'=2,'core'=2] {'core'}, dimensions={0}, use_global_device_ids=true | all-gather | bytes 786432 | tf_op jit(solution)/shard_map/all_gather | solution.py:99
  101.0 3.7 %collective-permute-start.3 = (bf16[16,4096]{1,0:T(8,128)(2,1)S(1)}, bf16[16,4096]{1,0:T(8,128)(2,1)S(1)}, u32[]{:S(2)}, u32[]{:S(2)}) collective-permute-start(bf16[16,4096]{1,0:T(8,128)(2,1)S(1)} %get-tuple-element.10), channel_id=1, source_target_pairs={{0,4},{4,8},{8,12},{12,0},{1,5},{5,9},{9,13},{13,1},{2,6},{6,10},{... | collective-permute-start | bytes 393224 | tf_op jit(solution)/shard_map/ppermute | solution.py:108
  104.7 3.1 %collective-permute-start.5 = (bf16[16,4096]{1,0:T(8,128)(2,1)S(1)}, bf16[16,4096]{1,0:T(8,128)(2,1)S(1)}, u32[]{:S(2)}, u32[]{:S(2)}) collective-permute-start(bf16[16,4096]{1,0:T(8,128)(2,1)S(1)} %get-tuple-element.11), channel_id=1, source_target_pairs={{0,12},{4,0},{8,4},{12,8},{1,13},{5,1},{9,5},{13,9},{2,14},{6,2},{... | collective-permute-start | bytes 393224 | tf_op jit(solution)/shard_map/ppermute | solution.py:108
  107.8 3.7 %collective-permute-start.4 = (bf16[16,4096]{1,0:T(8,128)(2,1)S(1)}, bf16[16,4096]{1,0:T(8,128)(2,1)S(1)}, u32[]{:S(2)}, u32[]{:S(2)}) collective-permute-start(bf16[16,4096]{1,0:T(8,128)(2,1)S(1)} %get-tuple-element.12), channel_id=1, source_target_pairs={{0,8},{4,12},{8,0},{12,4},{1,9},{5,13},{9,1},{13,5},{2,10},{6,14},... | collective-permute-start | bytes 393224 | tf_op jit(solution)/shard_map/ppermute | solution.py:108
  111.5 4.1 %collective-permute-done.4 = bf16[16,4096]{1,0:T(8,128)(2,1)S(1)} collective-permute-done((bf16[16,4096]{1,0:T(8,128)(2,1)S(1)}, bf16[16,4096]{1,0:T(8,128)(2,1)S(1)}, u32[]{:S(2)}, u32[]{:S(2)}) %collective-permute-start.4) | collective-permute-done | bytes 131104 | tf_op jit(solution)/shard_map/ppermute | solution.py:108
  115.7 8.1 %all_gather.32 = bf16[2,8,4096]{2,1,0:T(8,128)(2,1)S(1)} all-gather(bf16[1,8,4096]{2,1,0:T(8,128)(2,1)S(1)} %dynamic-slice_convert_fusion), channel_id=1, replica_groups=mesh['ylo'=4,'z'=8,'x'=4,'yhi'=2,'core'=2] {'yhi'}, dimensions={0}, use_global_device_ids=true | all-gather | bytes 196608 | tf_op jit(solution)/shard_map/all_gather | solution.py:113
  123.8 0.6 fusion.10
  124.5 5.7 %all-to-all-done.2 = bf16[8,896,128]{2,1,0:T(8,128)(2,1)} async-done(((bf16[8,896,128]{2,1,0:T(8,128)(2,1)}), bf16[8,896,128]{2,1,0:T(8,128)(2,1)}, u32[]{:S(2)}, u32[]{:S(2)}) %all-to-all-start.2) | async-done | bytes 1835040 | tf_op jit(solution)/shard_map/all_to_all | solution.py:82
  130.2 2.6 %convert_reduce_fusion = f32[896,128]{1,0:T(8,128)} fusion(bf16[8,896,128]{2,1,0:T(8,128)(2,1)} %all-to-all-done.2), kind=kLoop, calls=%fused_computation.4 | loop fusion | flops 1720320 | bytes 2293760 | tf_op jit(solution)/shard_map/reduce_sum | solution.py:117
  (44 shorter events, 1.7 us)
Async XLA Ops:
  1.5 17.6 %collective-permute-start = (bf16[16,4096]{1,0:T(8,128)(2,1)S(1)}, bf16[16,4096]{1,0:T(8,128)(2,1)S(1)}, u32[]{:S(2)}, u32[]{:S(2)}) collective-permute-start(bf16[16,4096]{1,0:T(8,128)(2,1)S(1)} %pad_maximum_fusion.3), channel_id=1, source_target_pairs={{0,2},{2,0},{1,3},{3,1},{4,6},{6,4},{5,7},{7,5},{8,10},{10,8},{9,1... | collective-permute-start | bytes 393224 | tf_op jit(solution)/shard_map/ppermute | solution.py:24
  11.4 25.0 %all-to-all-start = ((bf16[16,8,1024]{2,1,0:T(8,128)(2,1)}), bf16[16,8,1024]{2,1,0:T(8,128)(2,1)S(1)}, u32[]{:S(2)}, u32[]{:S(2)}) async-start(bf16[16,8,1024]{2,1,0:T(8,128)(2,1)} %bitcast.2), calls=%async_computation | async-start | bytes 524288 | tf_op jit(solution)/shard_map/all_to_all | solution.py:54
  30.6 11.1 %collective-permute-start.1 = (bf16[4,1,16,4096]{3,2,1,0:T(8,128)(2,1)S(1)}, bf16[4,1,16,4096]{3,2,1,0:T(8,128)(2,1)S(1)}, u32[]{:S(2)}, u32[]{:S(2)}) collective-permute-start(bf16[4,1,16,4096]{3,2,1,0:T(8,128)(2,1)S(1)} %bitcast.75), channel_id=1, source_target_pairs={{0,1},{1,0},{2,3},{3,2},{4,5},{5,4},{6,7},{7,6},{8,9},{9,8},{10,11... | collective-permute-start | bytes 1572872 | tf_op jit(solution)/shard_map/ppermute | solution.py:24
  38.2 29.6 %all-to-all-start.1 = ((bf16[4,3,16,4096]{3,2,1,0:T(8,128)(2,1)}), bf16[4,3,16,4096]{3,2,1,0:T(8,128)(2,1)S(1)}, u32[]{:S(2)}, u32[]{:S(2)}) async-start(bf16[4,3,16,4096]{3,2,1,0:T(8,128)(2,1)} %broadcast_in_dim.15), calls=%async_computation.1 | async-start | bytes 3145728 | tf_op jit(solution)/shard_map/all_to_all | solution.py:33
  41.7 4.7 %slice-start.2 = ((s8[7340032]{0:T(1024)(128)(4,1)}), s8[4194304]{0:T(1024)(128)(4,1)S(1)}, s32[]{:S(2)}) async-start(s8[7340032]{0:T(1024)(128)(4,1)} %bitcast.66), calls=%async_computation.5 | async-start | bytes 8388608
  41.9 5.2 %slice-start.3 = ((s8[7340032]{0:T(1024)(128)(4,1)}), s8[3145728]{0:T(1024)(128)(4,1)S(1)}, s32[]{:S(2)}) async-start(s8[7340032]{0:T(1024)(128)(4,1)} %bitcast.66), calls=%async_computation.6 | async-start | bytes 6291456
  47.0 2.1 %copy-start = (f32[128,896]{1,0:T(8,128)}, f32[128,896]{1,0:T(8,128)S(1)}, u32[]{:S(2)}) copy-start(f32[128,896]{1,0:T(8,128)S(1)} %fusion.15) | copy-start | bytes 1376260
  72.3 11.7 %collective-permute-start.2 = (bf16[4,1,16,4096]{3,2,1,0:T(8,128)(2,1)}, bf16[4,1,16,4096]{3,2,1,0:T(8,128)(2,1)}, u32[]{:S(2)}, u32[]{:S(2)}) collective-permute-start(bf16[4,1,16,4096]{3,2,1,0:T(8,128)(2,1)} %slice.36), channel_id=1, source_target_pairs={{0,1},{1,0},{2,3},{3,2},{4,5},{5,4},{6,7},{7,6},{8,9},{9,8},{10,11... | collective-permute-start | bytes 1572872 | tf_op jit(solution)/shard_map/ppermute | solution.py:24
  76.0 15.2 %slice-start = ((s8[7340032]{0:T(1024)(128)(4,1)}), s8[3145728]{0:T(1024)(128)(4,1)S(1)}, s32[]{:S(2)}) async-start(s8[7340032]{0:T(1024)(128)(4,1)} %bitcast.64), calls=%async_computation.3 | async-start | bytes 6291456
  76.0 54.2 %all-to-all-start.2 = ((bf16[8,896,128]{2,1,0:T(8,128)(2,1)}), bf16[8,896,128]{2,1,0:T(8,128)(2,1)}, u32[]{:S(2)}, u32[]{:S(2)}) async-start(bf16[8,896,128]{2,1,0:T(8,128)(2,1)} %bitcast.72), calls=%async_computation.2 | async-start | bytes 3670016 | tf_op jit(solution)/shard_map/all_to_all | solution.py:82
  84.0 7.1 %copy-start.1 = (f32[128,896]{1,0:T(8,128)S(1)}, f32[128,896]{1,0:T(8,128)}, u32[]{:S(2)}) copy-start(f32[128,896]{1,0:T(8,128)} %copy-done) | copy-start | bytes 1376260
  84.0 7.1 %copy-start.2 = (f32[128,896]{1,0:T(8,128)S(1)}, f32[128,896]{1,0:T(8,128)}, u32[]{:S(2)}) copy-start(f32[128,896]{1,0:T(8,128)} %get-tuple-element.24) | copy-start | bytes 1376260
  85.4 5.7 %slice-start.1 = ((s8[7340032]{0:T(1024)(128)(4,1)}), s8[4194304]{0:T(1024)(128)(4,1)S(1)}, s32[]{:S(2)}) async-start(s8[7340032]{0:T(1024)(128)(4,1)} %bitcast.64), calls=%async_computation.4 | async-start | bytes 8388608
  85.5 8.2 %slice-start.4 = ((s8[7340032]{0:T(1024)(128)(4,1)}), s8[4194304]{0:T(1024)(128)(4,1)S(1)}, s32[]{:S(2)}) async-start(s8[7340032]{0:T(1024)(128)(4,1)} %bitcast.68), calls=%async_computation.7 | async-start | bytes 8388608
  91.2 2.5 %slice-start.5 = ((s8[7340032]{0:T(1024)(128)(4,1)}), s8[3145728]{0:T(1024)(128)(4,1)S(1)}, s32[]{:S(2)}) async-start(s8[7340032]{0:T(1024)(128)(4,1)} %bitcast.68), calls=%async_computation.8 | async-start | bytes 6291456
  101.0 10.5 %collective-permute-start.3 = (bf16[16,4096]{1,0:T(8,128)(2,1)S(1)}, bf16[16,4096]{1,0:T(8,128)(2,1)S(1)}, u32[]{:S(2)}, u32[]{:S(2)}) collective-permute-start(bf16[16,4096]{1,0:T(8,128)(2,1)S(1)} %get-tuple-element.10), channel_id=1, source_target_pairs={{0,4},{4,8},{8,12},{12,0},{1,5},{5,9},{9,13},{13,1},{2,6},{6,10},{... | collective-permute-start | bytes 393224 | tf_op jit(solution)/shard_map/ppermute | solution.py:108
  104.7 6.8 %collective-permute-start.5 = (bf16[16,4096]{1,0:T(8,128)(2,1)S(1)}, bf16[16,4096]{1,0:T(8,128)(2,1)S(1)}, u32[]{:S(2)}, u32[]{:S(2)}) collective-permute-start(bf16[16,4096]{1,0:T(8,128)(2,1)S(1)} %get-tuple-element.11), channel_id=1, source_target_pairs={{0,12},{4,0},{8,4},{12,8},{1,13},{5,1},{9,5},{13,9},{2,14},{6,2},{... | collective-permute-start | bytes 393224 | tf_op jit(solution)/shard_map/ppermute | solution.py:108
  107.8 7.9 %collective-permute-start.4 = (bf16[16,4096]{1,0:T(8,128)(2,1)S(1)}, bf16[16,4096]{1,0:T(8,128)(2,1)S(1)}, u32[]{:S(2)}, u32[]{:S(2)}) collective-permute-start(bf16[16,4096]{1,0:T(8,128)(2,1)S(1)} %get-tuple-element.12), channel_id=1, source_target_pairs={{0,8},{4,12},{8,0},{12,4},{1,9},{5,13},{9,1},{13,5},{2,10},{6,14},... | collective-permute-start | bytes 393224 | tf_op jit(solution)/shard_map/ppermute | solution.py:108
